TPU v7x, 32 devices: a whole 2x2x4 slice. The times are simulated.
32 devices in a mesh: dp: 8 (over z, y), tensor: 4 (over x, core).
Axes of the slice: x: 2, y: 2, z: 4, core: 2. Of those that a mesh axis runs over, the one named last changes fastest.
Arguments:
- block_input: bfloat16 [4, 8192, 512], P(None, 'dp'), may hold values from -6 to 6
- cotangent: bfloat16 [4, 8192, 512], P(None, 'dp'), may hold values from -6 to 6
- source: int32 [4, 8192], replicated, may hold values from 0 to 8191, as said below
- seq_lengths: int32 [4, 8, 3], P(None, 'dp'), may hold values from 1 to 682, 1024 in all within a row
- qkv_weight: bfloat16 [3, 512, 512], P(None, None, 'tensor'), may hold values from -0.375 to 0.375
- qv_bias: bfloat16 [2, 512], P(None, 'tensor'), may hold values from -3 to 3
- out_weight: bfloat16 [512, 512], P('tensor'), may hold values from -0.75 to 0.75
- out_bias: bfloat16 [512], replicated, may hold values from -3 to 3
- up_weight: bfloat16 [512, 2048], P(None, 'tensor'), may hold values from -0.25 to 0.25
- up_bias: bfloat16 [2048], P('tensor'), may hold values from -3 to 3
- down_weight: bfloat16 [2048, 512], P('tensor'), may hold values from -0.25 to 0.25
- down_bias: bfloat16 [512], replicated, may hold values from -3 to 3
- rezero_alphas: float32 [2], replicated, may hold values from 0.2 to 0.45
Outputs:
- layer_output: float32 [4, 8192, 512], P(None, 'dp')
- input_grad: float32 [4, 8192, 512], P(None, 'dp')
- qkv_weight_grad: float32 [3, 512, 512], P(None, None, 'tensor')
- qv_bias_grad: float32 [2, 512], P(None, 'tensor')
- out_weight_grad: float32 [512, 512], P('tensor')
- out_bias_grad: float32 [512], replicated
- up_weight_grad: float32 [512, 2048], P(None, 'tensor')
- up_bias_grad: float32 [2048], P('tensor')
- down_weight_grad: float32 [2048, 512], P('tensor')
- down_bias_grad: float32 [512], replicated
- alphas_grad: float32 [2], replicated
Inputs may be any that keep to these rules, and one draw needn't show every extreme that they name: In each micro-batch source is a permutation of the input rows; the 1024 rows of one device go to every group in equal numbers, 128 each. `seq_lengths`: each row of 3 lengths sums to 1024.
All inputs are finite; a program needn't handle non-finite values.
Results may differ from a plain program's by a relative error of at most 0.011.
The roundings to bfloat16 on the way count: a program that leaves them out, or rounds other values in their place, can miss the bound.
Values may be sent and summed in bfloat16 or wider, within the bound.
No kernel may reach another device: no remote copies, remote signals or barrier semaphores. Data moves between devices by JAX's collectives and lax.ppermute only.
A program may use at most 256 MiB of HBM per device.

v0:
```python
import functools

import jax
import jax.numpy as jnp
from jax import lax
from jax.experimental import pallas as pl
from jax.experimental.pallas import tpu as pltpu
from jax.sharding import PartitionSpec as P

HEAD_SIZE = 64
LANES = 128
QT = 256
FT = 512
BF = jnp.bfloat16
F32 = jnp.float32
C = {"route": 6, "attend": 19, "forward": 5, "feed": 19, "back": 11, "halve": 1, "part": 5, "settle": 1, "last": 20, "weight": 0.2, "widen": 5, "spread": 3}
I32 = jnp.int32
NEG = -1e30
VMEM_LIMIT = 56 * 1024 * 1024
GELU_A = 0.7978845608028654
GELU_B = 0.044715

NN = (((1,), (0,)), ((), ()))
NT = (((1,), (1,)), ((), ()))
TN = (((0,), (0,)), ((), ()))


def dot(a, b, dims=NN):
    return lax.dot_general(a, b, dims, preferred_element_type=F32)


def iota(shape, dim):
    return lax.broadcasted_iota(I32, shape, dim)


def params(limit=VMEM_LIMIT):
    return pltpu.CompilerParams(vmem_limit_bytes=limit)


def cost(flops, nbytes, trans=0):
    return pl.CostEstimate(flops=int(flops), bytes_accessed=int(nbytes), transcendentals=int(trans))


def vmem(n):
    return [pl.BlockSpec(memory_space=pltpu.VMEM)] * n


def smem():
    return pl.BlockSpec(memory_space=pltpu.SMEM)


def one_hot_rows(row, count):
    return (iota((count, row.shape[1]), 0) == row).astype(F32).astype(BF)


def one_hot_cols(col, count):
    return (iota((col.shape[0], count), 1) == col).astype(F32).astype(BF)


def route_kernel(groups, ids_ref, src_ref, x_ref, xs_ref, srow_ref, scol_ref, hot_ref):
    me, micro = ids_ref[0], ids_ref[1]
    rows = x_ref.shape[1]
    chunks = rows // LANES
    share = rows // groups
    sub_hi = iota((chunks, rows), 0)
    sub_lo = iota((LANES, rows), 0)

    def gather_group(g, total):
        value = src_ref[pl.ds(micro, 1), pl.ds(pl.multiple_of(g * rows, LANES), rows)] - me * rows
        inside = (value >= 0) & (value < rows)
        high = jnp.where(inside, value // LANES, -1)
        low = jnp.where(inside, value % LANES, -1)
        hot_high = jnp.where(high == sub_hi, (g + 1).astype(F32), 0.0).astype(BF)
        hot_low = (low == sub_lo).astype(F32).astype(BF)
        return total + dot(hot_high, hot_low, NT)

    dest = lax.fori_loop(0, groups, gather_group, jnp.zeros((chunks, LANES), F32)).astype(I32) - 1
    before = (iota((LANES, LANES), 0) < iota((LANES, LANES), 1)).astype(F32).astype(BF)
    width = max(groups, 8)
    carry = jnp.zeros((width, 1), F32)
    for c in range(chunks):
        g_row = dest[c : c + 1, :]
        hot = (iota((width, LANES), 0) == g_row).astype(F32)
        ranks = dot(hot.astype(BF), before) + carry
        carry = carry + jnp.sum(hot, axis=1, keepdims=True)
        place = g_row * share + jnp.sum(hot * ranks, axis=0, keepdims=True).astype(I32)
        srow_ref[c : c + 1, :] = place
        spread = jnp.broadcast_to(place.astype(F32), (LANES, LANES))
        scol_ref[c * LANES : (c + 1) * LANES, :] = spread.T.astype(I32)
        hot_ref[:, c * LANES : (c + 1) * LANES] = one_hot_rows(place, rows)
    xs_ref[...] = dot(hot_ref[...], x_ref[0]).astype(BF)


def second_kernel(ids_ref, src_ref, g_ref, srow_ref, gs_ref, arow_ref, acol_ref, hot_ref):
    me, micro = ids_ref[0], ids_ref[1]
    rows = g_ref.shape[1]
    for c in range(rows // LANES):
        hot_ref[:, c * LANES : (c + 1) * LANES] = one_hot_rows(srow_ref[c : c + 1, :], rows)
    gs_ref[...] = dot(hot_ref[...], g_ref[0]).astype(BF)
    own = src_ref[pl.ds(micro, 1), pl.ds(pl.multiple_of(me * rows, LANES), rows)].astype(F32)
    for c in range(rows // LANES):
        piece = own[:, c * LANES : (c + 1) * LANES]
        column = jnp.broadcast_to(piece, (LANES, LANES)).T[:, 0:1]
        count = jnp.sum((own < column).astype(F32), axis=1, keepdims=True)
        spread = jnp.broadcast_to(count, (LANES, LANES))
        acol_ref[c * LANES : (c + 1) * LANES, :] = spread.astype(I32)
        arow_ref[0:1, c * LANES : (c + 1) * LANES] = spread.T[0:1, :].astype(I32)


def starts_of(len_ref, index):
    start = jnp.zeros_like(index)
    first = jnp.int32(0)
    for j in range(len_ref.shape[0] - 1):
        first = first + len_ref[j]
        start = jnp.where(index >= first, first, start)
    return start


class Copies:
    def __init__(self, sems):
        self.sems, self.used, self.left = sems, 0, []

    def start(self, source, target):
        copy = pltpu.make_async_copy(source, target, self.sems.at[self.used])
        self.used += 1
        copy.start()
        return copy

    def send(self, source, target):
        self.left.append(self.start(source, target))

    def finish(self):
        for copy in self.left:
            copy.wait()


def wait_all(copies):
    for copy in copies:
        copy.wait()


def attend_kernel(
    ids_ref, len_ref, alpha_ref, b0_ref, b1_ref, b2_ref, b3_ref, ob_ref, acol_ref,
    arr_any, wa0_any, wa1_any, wa2_any, wa3_any, wo0_any, wo1_any, wo2_any, wo3_any,
    l_ref, x_any, q_any, k_any, v_any, o_any, h_any, low_any, attn_any,
    sems, arr_ref, wcat_ref, wo_ref, bias_ref, hot_ref, x_ref, q_ref, k_ref, v_ref, ob16_ref, h_ref, low_ref, attn_ref,
):
    rows, width = arr_ref.shape
    lanes = wo0_any.shape[0]
    pieces = width // lanes
    heads = lanes // HEAD_SIZE
    tensor = ids_ref[1]
    copies = Copies(sems)
    first = copies.start(arr_any, arr_ref)
    weights, later = [], []
    for j, (wa, wo, b) in enumerate(
        ((wa0_any, wo0_any, b0_ref), (wa1_any, wo1_any, b1_ref), (wa2_any, wo2_any, b2_ref), (wa3_any, wo3_any, b3_ref))
    ):
        place = pl.multiple_of(lax.bitwise_xor(tensor, j) * lanes, LANES)
        for c in range(3):
            weights.append(copies.start(wa.at[c], wcat_ref.at[:, pl.ds(c * width + place, lanes)]))
        later.append(copies.start(wo, wo_ref.at[pl.ds(place, lanes), :]))
        bias_ref[:, pl.ds(place, lanes)] = b[...].astype(F32)
    hot_ref[...] = one_hot_cols(acol_ref[:, 0:1], rows)
    first.wait()
    x_ref[...] = dot(hot_ref[...], arr_ref[...]).astype(BF)
    copies.send(x_ref, x_any)
    wait_all(weights)
    q_ref[...] = (dot(x_ref[...], wcat_ref[:, 0:width]) + bias_ref[0:1, :]).astype(BF) * jnp.asarray(HEAD_SIZE**-0.5, BF)
    k_ref[...] = dot(x_ref[...], wcat_ref[:, width : 2 * width]).astype(BF)
    v_ref[...] = (dot(x_ref[...], wcat_ref[:, 2 * width :]) + bias_ref[1:2, :]).astype(BF)
    copies.send(q_ref, q_any)
    copies.send(k_ref, k_any)
    copies.send(v_ref, v_any)
    tiles = rows // QT
    lane = iota((QT, lanes), 1) // HEAD_SIZE
    masks = []
    for i in range(tiles):
        q_index = i * QT + iota((QT, 1), 0)
        k_index = iota((QT, (i + 1) * QT), 1)
        masks.append((k_index >= starts_of(len_ref, q_index)) & (k_index <= q_index))

    def scores_of(p, i, e):
        q = q_ref[i * QT : (i + 1) * QT, p * lanes : (p + 1) * lanes]
        return dot(jnp.where(lane == e, q, jnp.zeros_like(q)), k_ref[0 : (i + 1) * QT, p * lanes : (p + 1) * lanes], NT)

    items = [(p, i, e) for i in range(tiles) for p in range(pieces) for e in range(heads)]
    ahead = scores_of(*items[0])
    mixed = logs = None
    for step, (p, i, e) in enumerate(items):
        now = ahead
        if step + 1 < len(items):
            ahead = scores_of(*items[step + 1])
        scores = jnp.where(masks[i], now, NEG)
        top = jnp.max(scores, axis=1, keepdims=True)
        weights = jnp.exp(scores - top)
        total = jnp.sum(weights, axis=1, keepdims=True)
        low = (weights * (1.0 / total)).astype(BF)
        out = dot(low, v_ref[0 : (i + 1) * QT, p * lanes : (p + 1) * lanes])
        head = p * heads + e
        log_total = top + jnp.log(total)
        logs = jnp.where(iota((QT, LANES), 1) == head, log_total, 0.0 if head == 0 else logs)
        mixed = out if e == 0 else jnp.where(lane == e, out, mixed)
        if e == heads - 1:
            ob16_ref[i * QT : (i + 1) * QT, p * lanes : (p + 1) * lanes] = mixed.astype(BF)
        if head == pieces * heads - 1:
            l_ref[:, i * QT : (i + 1) * QT] = logs.T[0 : pieces * heads, :]
            if i == 0:
                wait_all(later)
            span = slice(i * QT, (i + 1) * QT)
            copies.send(ob16_ref.at[span], o_any.at[span])
            attn = dot(ob16_ref[span, :], wo_ref[...]) + ob_ref[...].astype(F32)
            hidden = x_ref[span, :].astype(F32) + alpha_ref[0] * attn
            attn_ref[span, :] = attn
            h_ref[span, :] = hidden
            low_ref[span, :] = hidden.astype(BF)
            copies.send(attn_ref.at[span], attn_any.at[span])
            copies.send(h_ref.at[span], h_any.at[span])
            copies.send(low_ref.at[span], low_any.at[span])
    copies.finish()


def forward_kernel(
    alpha_ref, b0_ref, b1_ref, b2_ref, b3_ref, db_ref, arow_ref,
    low_any, h_any, wu0_any, wu1_any, wu2_any, wu3_any, wd0_any, wd1_any, wd2_any, wd3_any,
    ys_any, act_any, slope_any, f_any,
    sems, low_ref, h_ref, wu_ref, wd_ref, act_ref, slope_ref, f_ref, y_ref, hot_ref, ys_ref,
):
    rows, width = low_ref.shape
    units = wu0_any.shape[1]
    copies = Copies(sems)
    first = copies.start(low_any, low_ref)
    up, down = [], []
    for j, wu in enumerate((wu0_any, wu1_any, wu2_any, wu3_any)):
        up.append(copies.start(wu, wu_ref.at[:, j * units : (j + 1) * units]))
    for j, wd in enumerate((wd0_any, wd1_any, wd2_any, wd3_any)):
        down.append(copies.start(wd, wd_ref.at[j * units : (j + 1) * units, :]))
    hidden = copies.start(h_any, h_ref)
    biases = []
    for b in (b0_ref, b1_ref, b2_ref, b3_ref):
        tail = b[...].astype(F32)
        biases.append(jnp.concatenate([tail[2 + n : 3 + n, :] for n in range(units // LANES)], axis=1))
    first.wait()
    items = [(j, m) for j in range(len(biases)) for m in range(rows // FT)]

    def z_of(j, m):
        if m == 0:
            up[j].wait()
        return dot(low_ref[m * FT : (m + 1) * FT, :], wu_ref[:, j * units : (j + 1) * units])

    ahead = z_of(*items[0])
    for step, (j, m) in enumerate(items):
        z = ahead + biases[j]
        if step + 1 < len(items):
            ahead = z_of(*items[step + 1])
        square = z * z
        tanh = jnp.tanh(z * (GELU_A + (GELU_A * GELU_B) * square))
        half = 0.5 * z
        rise = 0.5 + 0.5 * tanh
        span = (slice(m * FT, (m + 1) * FT), slice(j * units, (j + 1) * units))
        act_ref[span] = (z * rise).astype(BF)
        slope_ref[span] = rise + half * (1.0 - tanh * tanh) * (GELU_A + (3 * GELU_A * GELU_B) * square)
        if m == rows // FT - 1:
            copies.send(act_ref.at[:, span[1]], act_any.at[:, span[1]])
            copies.send(slope_ref.at[:, span[1]], slope_any.at[:, span[1]])
    wait_all(down)
    hidden.wait()
    for m in range(rows // FT):
        span = slice(m * FT, (m + 1) * FT)
        branch = dot(act_ref[span, :], wd_ref[...]) + db_ref[...].astype(F32)
        f_ref[span, :] = branch
        copies.send(f_ref.at[span], f_any.at[span])
        y_ref[span, :] = (h_ref[span, :] + alpha_ref[1] * branch).astype(BF)
        hot_ref[span, :] = (iota((FT, rows), 0) + m * FT == arow_ref[0:1, :]).astype(F32).astype(BF)
    for m in range(rows // FT):
        span = slice(m * FT, (m + 1) * FT)
        ys_ref[span, :] = dot(hot_ref[span, :], y_ref[...]).astype(BF)
        copies.send(ys_ref.at[span], ys_any.at[span])
    copies.finish()


def feed_kernel(
    ids_ref, alpha_ref, acol_ref,
    arr_any, wu0_any, wu1_any, wu2_any, wu3_any, wd0_any, wd1_any, wd2_any, wd3_any,
    wo0_any, wo1_any, wo2_any, wo3_any, act_any, slope_any, low_any, f_any, attn_any, o_any,
    small_ref, go_any, gh_any, keep_any, send_any,
    sems, arr_ref, wu_ref, wd_ref, wo_ref, act_ref, slope_ref, low_ref, f_ref, attn_ref, o_ref,
    hot_ref, g_ref, gf_ref, gz_ref, gh_ref, ga_ref, go_ref, keep_ref, part_ref, w_ref,
):
    me, tensor = ids_ref[0], ids_ref[1]
    rows, width = low_ref.shape
    units = wu0_any.shape[1]
    lanes = wo0_any.shape[0]
    blocks = part_ref.shape[1]
    own = me % blocks
    copies = Copies(sems)
    first = copies.start(arr_any, arr_ref)
    down, slopes, up, later = [], [], [], []
    for j, wd in enumerate((wd0_any, wd1_any, wd2_any, wd3_any)):
        span = slice(j * units, (j + 1) * units)
        down.append(copies.start(wd, wd_ref.at[span, :]))
        slopes.append(copies.start(slope_any.at[:, span], slope_ref.at[:, span]))
    for j, wu in enumerate((wu0_any, wu1_any, wu2_any, wu3_any)):
        up.append(copies.start(wu, wu_ref.at[:, j * units : (j + 1) * units]))
    lowed = copies.start(low_any, low_ref)
    acted = copies.start(act_any, act_ref)
    for j, wo in enumerate((wo0_any, wo1_any, wo2_any, wo3_any)):
        place = pl.multiple_of(lax.bitwise_xor(tensor, j) * lanes, LANES)
        later.append(copies.start(wo, wo_ref.at[pl.ds(place, lanes), :]))
    later.append(copies.start(attn_any, attn_ref))
    later.append(copies.start(o_any, o_ref))
    branched = copies.start(f_any, f_ref)
    hot_ref[...] = one_hot_cols(acol_ref[:, 0:1], rows)
    first.wait()
    for m in range(rows // FT):
        span = slice(m * FT, (m + 1) * FT)
        grad = dot(hot_ref[span, :], arr_ref[...])
        g_ref[span, :] = grad.astype(BF)
        gf_ref[span, :] = (alpha_ref[1] * grad).astype(BF)
    items = [(j, m) for j in range(len(up)) for m in range(rows // FT)]

    def ga_of(j, m):
        if m == 0:
            down[j].wait()
        return dot(gf_ref[m * FT : (m + 1) * FT, :], wd_ref[j * units : (j + 1) * units, :], NT)

    ahead = ga_of(*items[0])
    for step, (j, m) in enumerate(items):
        now = ahead
        if step + 1 < len(items):
            ahead = ga_of(*items[step + 1])
        if m == 0:
            slopes[j].wait()
        span = (slice(m * FT, (m + 1) * FT), slice(j * units, (j + 1) * units))
        gz_ref[span] = (now * slope_ref[span]).astype(BF)
    wait_all(up)
    wait_all(later)
    gh_sum = attn_sum = jnp.zeros((1, width), F32)
    for m in range(rows // FT):
        span = slice(m * FT, (m + 1) * FT)
        grad_hidden = g_ref[span, :].astype(F32) + dot(gz_ref[span, :], wu_ref[...], NT)
        gh_ref[span, :] = grad_hidden
        copies.send(gh_ref.at[span], gh_any.at[span])
        ga = (alpha_ref[0] * grad_hidden).astype(BF)
        ga_ref[span, :] = ga
        gh_sum = gh_sum + jnp.sum(ga.astype(F32), axis=0, keepdims=True)
        attn_sum = attn_sum + jnp.sum(grad_hidden * attn_ref[span, :], axis=0, keepdims=True)
    for m in range(rows // FT):
        span = slice(m * FT, (m + 1) * FT)
        go = dot(ga_ref[span, :], wo_ref[...], NT).astype(BF)
        go_ref[span, :] = go
        copies.send(go_ref.at[span], go_any.at[span])

    def place(j, first_row, value):
        count = value.shape[0] // blocks
        out = keep_ref if j % 2 == 0 else part_ref
        for b in range(blocks):
            out[j // 2, lax.bitwise_xor(own, b), first_row : first_row + count, :] = value[b * count : (b + 1) * count].astype(out.dtype)

    lowed.wait()
    acted.wait()
    low_t = low_ref[...].T
    gf_t = gf_ref[...].T
    o_t = o_ref[...].T
    w_ref[...] = dot(o_t, ga_ref[...])
    edge = (width + units) // blocks
    for j in range(len(up)):
        span = slice(j * units, (j + 1) * units)
        place(j, 0, dot(low_t, gz_ref[:, span]))
        place(j, width // blocks, dot(gf_t, act_ref[:, span]))
        at = pl.multiple_of(lax.bitwise_xor(tensor, j) * lanes, LANES)
        place(j, edge, w_ref[pl.ds(at, lanes), :])
        held, out = (keep_ref, keep_any) if j % 2 == 0 else (part_ref, send_any)
        copies.send(held.at[j // 2], out.at[j // 2])
        small_ref[pl.ds(lax.bitwise_xor(tensor, j), 1), :] = jnp.sum(gz_ref[:, span].astype(F32), axis=0, keepdims=True)
    branched.wait()
    small_ref[4:5, :] = gh_sum
    small_ref[5:6, :] = jnp.sum(gf_ref[...].astype(F32), axis=0, keepdims=True)
    small_ref[6:7, :] = attn_sum
    small_ref[7:8, :] = jnp.sum(g_ref[...].astype(F32) * f_ref[...], axis=0, keepdims=True)
    copies.finish()


def starts_of(len_ref, index):
    start = jnp.zeros_like(index)
    first = jnp.int32(0)
    for j in range(len_ref.shape[0] - 1):
        first = first + len_ref[j]
        start = jnp.where(index >= first, first, start)
    return start


def back_kernel(
    first_pair, len_ref, l_ref, q_any, k_any, v_any, go_any,
    grad_any,
    sems, q_ref, k_ref, v_ref, go_ref, grad_ref, gk_ref, gv_ref,
):
    rows, width = q_ref.shape
    lanes = 2 * HEAD_SIZE
    heads = 2
    pairs = width // lanes
    scale = HEAD_SIZE**-0.5
    copies = Copies(sems)
    columns = slice(first_pair * lanes, first_pair * lanes + width)
    ins = [copies.start(a.at[:, columns], r) for a, r in ((q_any, q_ref), (k_any, k_ref), (v_any, v_ref), (go_any, go_ref))]
    tiles = rows // QT
    lane = iota((QT, lanes), 1) // HEAD_SIZE
    masks = []
    for i in range(tiles):
        q_index = i * QT + iota((1, QT), 1)
        k_index = iota(((i + 1) * QT, QT), 0)
        masks.append((k_index >= starts_of(len_ref, q_index)) & (k_index <= q_index))
    wait_all(ins)
    items = [(p, i, e) for p in range(pairs) for i in reversed(range(tiles)) for e in range(heads)]

    def pick(ref, p, i, e):
        value = ref[i * QT : (i + 1) * QT, p * lanes : (p + 1) * lanes]
        return jnp.where(lane == e, value, jnp.zeros_like(value))

    def both_of(p, i, e):
        pair = (slice(0, (i + 1) * QT), slice(p * lanes, (p + 1) * lanes))
        return dot(k_ref[pair], pick(q_ref, p, i, e), NT), dot(v_ref[pair], pick(go_ref, p, i, e), NT)

    ahead = both_of(*items[0])
    gq = None
    for step, (p, i, e) in enumerate(items):
        scores, grad_weights = ahead
        if step + 1 < len(items):
            ahead = both_of(*items[step + 1])
        head = (first_pair + p) * heads + e
        n = (i + 1) * QT
        weights = jnp.exp(jnp.where(masks[i], scores - l_ref[head : head + 1, i * QT : n], NEG))
        inner = jnp.sum(weights * grad_weights, axis=0, keepdims=True)
        grad_scores = (weights * (grad_weights - inner)).astype(BF)
        gv = dot(weights.astype(BF), pick(go_ref, p, i, e))
        gk = dot(grad_scores, pick(q_ref, p, i, e))
        if i == tiles - 1 and e == 0:
            gv_ref[...] = gv
            gk_ref[...] = gk
        else:
            gv_ref[0:n, :] += gv
            gk_ref[0:n, :] += gk
        gq_e = dot(grad_scores, k_ref[0:n, p * lanes : (p + 1) * lanes], TN)
        gq = gq_e if e == 0 else jnp.where(lane == e, gq_e, gq)
        if e == heads - 1:
            span = (slice(i * QT, n), slice(p * lanes, (p + 1) * lanes))
            grad_ref[(0, *span)] = (gq * scale).astype(BF)
            grad_ref[(1, *span)] = gk_ref[i * QT : n, :].astype(BF)
            grad_ref[(2, *span)] = gv_ref[i * QT : n, :].astype(BF)
            if i == 0:
                copies.send(grad_ref.at[:, :, p * lanes : (p + 1) * lanes], grad_any.at[:, :, p * lanes : (p + 1) * lanes])
    copies.finish()


def split_small(value, out_ref):
    chunks = value.shape[1] // LANES
    for c in range(chunks):
        left = value[:, c * LANES : (c + 1) * LANES]
        for k in range(2):
            term = left.astype(BF)
            first = (k * chunks + c) * 16
            out_ref[first : first + 16, :] = term
            left = left - term.astype(F32)


def join_small(ref, width):
    chunks = width // LANES
    parts = []
    for c in range(chunks):
        terms = [ref[(k * chunks + c) * 16 : (k * chunks + c + 1) * 16, :].astype(F32) for k in range(2)]
        parts.append(terms[0] + terms[1])
    return jnp.concatenate(parts, axis=1)


def last_kernel(
    ids_ref, arow_ref, grad_a_any, grad_b_any, gh_any, wa0_any, wa1_any, wa2_any, wa3_any,
    gxs_any,
    sems, grad_ref, gh_ref, wcat_ref, hot_ref, gx_ref, gxs_ref,
):
    tensor = ids_ref[1]
    rows, width = gx_ref.shape
    lanes = wa0_any.shape[2]
    half = width // 2
    copies = Copies(sems)
    grads, weights = [], []
    for c in range(3):
        for n, g in enumerate((grad_a_any, grad_b_any)):
            grads.append(copies.start(g.at[c], grad_ref.at[:, c * width + n * half : c * width + (n + 1) * half]))
    for j, wa in enumerate((wa0_any, wa1_any, wa2_any, wa3_any)):
        place = pl.multiple_of(lax.bitwise_xor(tensor, j) * lanes, LANES)
        for c in range(3):
            weights.append(copies.start(wa.at[c], wcat_ref.at[:, pl.ds(c * width + place, lanes)]))
    hidden = copies.start(gh_any, gh_ref)
    for m in range(rows // FT):
        hot_ref[m * FT : (m + 1) * FT, :] = (iota((FT, rows), 0) + m * FT == arow_ref[0:1, :]).astype(F32).astype(BF)
    wait_all(grads)
    wait_all(weights)
    hidden.wait()
    for m in range(rows // FT):
        span = slice(m * FT, (m + 1) * FT)
        gx_ref[span, :] = (gh_ref[span, :] + dot(grad_ref[span, :], wcat_ref[...], NT)).astype(BF)
    for m in range(rows // FT):
        span = slice(m * FT, (m + 1) * FT)
        gxs_ref[span, :] = dot(hot_ref[span, :], gx_ref[...]).astype(BF)
        copies.send(gxs_ref.at[span], gxs_any.at[span])
    copies.finish()


def weight_kernel(
    ids_ref, small1_ref, grad_a_any, grad_b_any, x_any,
    small_ref, keep_any, send_any,
    sems, grad_ref, x_ref, keep_ref, part_ref, w_ref, split_ref,
):
    tensor = ids_ref[1]
    rows, width = x_ref.shape
    lanes = keep_ref.shape[2]
    half = width // 2
    blocks = keep_ref.shape[0] // 2
    copies = Copies(sems)
    xs = copies.start(x_any, x_ref)
    grads = [
        [
            copies.start(g.at[c], grad_ref.at[:, c * width + n * half : c * width + (n + 1) * half])
            for n, g in enumerate((grad_a_any, grad_b_any))
        ]
        for c in range(3)
    ]
    xs.wait()
    x_t = x_ref[...].T
    count = width // blocks
    small_ref[0:8, :] = small1_ref[...]
    small_ref[8:16, :] = jnp.zeros((8, width), F32)
    for c in range(3):
        wait_all(grads[c])
        span = slice(c * width, (c + 1) * width)
        w_ref[:, span] = dot(x_t, grad_ref[:, span])
        if c != 1:
            row = 8 + c // 2
            small_ref[row : row + 1, :] = jnp.sum(grad_ref[:, span].astype(F32), axis=0, keepdims=True)
    for j in range(width // lanes):
        at = pl.multiple_of(lax.bitwise_xor(tensor, j) * lanes, LANES)
        held, out = (keep_ref, keep_any) if j % 2 == 0 else (part_ref, send_any)
        first = j // 2 * blocks
        for c in range(3):
            for b in range(blocks):
                held[first + b, c * count : (c + 1) * count, :] = w_ref[
                    b * count : (b + 1) * count, pl.ds(c * width + at, lanes)
                ].astype(held.dtype)
        copies.send(held.at[pl.ds(first, blocks)], out.at[pl.ds(first, blocks)])
    split_small(small_ref[...], split_ref)
    copies.send(split_ref, send_any.at[send_any.shape[0] - 1, 0 : split_ref.shape[0]])
    copies.finish()


def halve_kernel(pick, keep_ref, got_ref, next_ref, send_ref):
    here = there = 0
    for b in range(keep_ref.shape[0]):
        total = keep_ref[b] + got_ref[b].astype(F32)
        if pick(b):
            next_ref[here] = total
            here += 1
        else:
            send_ref[there] = total.astype(BF)
            there += 1


def halve_small_kernel(pick, keep_ref, small_ref, got_ref, next_ref, total_ref, send_ref):
    halve_kernel(pick, keep_ref, got_ref, next_ref, send_ref)
    total = small_ref[...] + join_small(got_ref.at[got_ref.shape[0] - 1], small_ref.shape[1])
    total_ref[...] = total
    split_small(total, send_ref.at[send_ref.shape[0] - 1])


def part_kernel(keep_ref, got_ref, *outs):
    for b in range(keep_ref.shape[0]):
        outs[b][...] = (keep_ref[b] + got_ref[b].astype(F32)).astype(outs[b].dtype)


def whole_small_kernel(keep_ref, small_ref, got_ref, send_ref, total_ref):
    rows = keep_ref.shape[1]
    total = small_ref[...] + join_small(got_ref.at[got_ref.shape[0] - 1], small_ref.shape[1])
    total_ref[...] = total
    for b in range(keep_ref.shape[0]):
        send_ref[b, 0:rows, :] = (keep_ref[b] + got_ref[b].astype(F32)).astype(BF)
        if b == 0:
            split_small(total, send_ref.at[0, rows:])
        else:
            send_ref[b, rows:, :] = send_ref[0, rows:, :]


def sum_kernel(own_ref, a_ref, b_ref, c_ref, out_ref):
    out_ref[...] = own_ref[...] + a_ref[...].astype(F32) + b_ref[...].astype(F32) + c_ref[...].astype(F32)


def pack_kernel(own1_ref, got_ref, packed_ref, total_ref):
    first = own1_ref[...]
    ways = own1_ref.shape[1] // got_ref.shape[2]
    rows, lanes = got_ref.shape[1] - 2 * 16 * ways, got_ref.shape[2]
    value = total = 0.0
    for b in range(got_ref.shape[0]):
        value = value + got_ref[b, 0:rows, :].astype(F32)
        total = total + join_small(got_ref.at[b, rows:], total_ref.shape[1])
    total_ref[...] = total
    edge = own1_ref.shape[0]
    packed_ref[0:edge, :] = first.astype(packed_ref.dtype)
    for c in range(ways):
        packed_ref[edge:, c * lanes : (c + 1) * lanes] = value[c * (rows // ways) : (c + 1) * (rows // ways)].astype(packed_ref.dtype)


def add_one_kernel(a_ref, b_ref, small_ref, other_ref, out_ref, total_ref):
    out_ref[...] = (a_ref[...].astype(F32) + b_ref[...].astype(F32)).astype(out_ref.dtype)
    total_ref[...] = small_ref[...] + other_ref[...]


def spread_kernel(count, ids_ref, small_ref, *refs):
    blocks = refs[:count]
    qkv_ref, qv_ref, out_ref, ob_ref, up_ref, ub_ref, down_ref, db_ref, alpha_ref, turned_ref, second_ref = refs[count:]
    me, tensor = ids_ref[0], ids_ref[1]
    lanes = out_ref.shape[0]
    for j, ref in enumerate(blocks):
        slot = lax.bitwise_xor(me % count, j)
        first = 0
        for out in (up_ref, turned_ref, out_ref):
            size = out.shape[0] // count
            out[pl.ds(pl.multiple_of(slot * size, 8), size), :] = ref[first : first + size, :].astype(F32)
            first += size
        size = qkv_ref.shape[1] // count
        rest = ref.shape[0] - first
        for c in range(ref.shape[1] // lanes):
            second_ref[c * rest : (c + 1) * rest, :] = ref[first:, c * lanes : (c + 1) * lanes].astype(F32)
        for c in range(3):
            qkv_ref[c, pl.ds(pl.multiple_of(slot * size, 8), size), :] = second_ref[c * size : (c + 1) * size, :]
    down_ref[...] = turned_ref[...].T
    ub_ref[...] = small_ref[pl.ds(tensor, 1), :]
    ob_ref[...] = small_ref[4:5, :]
    db_ref[...] = small_ref[5:6, :]
    qv_ref[...] = small_ref[8:10, pl.ds(pl.multiple_of(tensor * lanes, LANES), lanes)]
    sums = jnp.sum(small_ref[6:8, :], axis=1, keepdims=True)
    spread = jnp.concatenate([sums, jnp.zeros((6, 1), F32)], axis=0)
    alpha_ref[...] = jnp.broadcast_to(spread, (8, LANES))


def widen_kernel(first, ids_ref, a_any, b_any, *refs):
    out_any, sems, wide_ref, low_ref = refs[-4:]
    rows = low_ref.shape[1]
    copies = Copies(sems)
    ins = [copies.start(a, low_ref.at[n]) for n, a in enumerate((a_any, b_any))]
    half = rows // 2
    for n in range(2):
        ins[n].wait()
        slot = lax.bitwise_xor(ids_ref[1], first + n)
        for m in range(2):
            span = slice(m * half, (m + 1) * half)
            wide_ref[n, span, :] = low_ref[n, span, :].astype(F32)
            copies.send(wide_ref.at[n, span], out_any.at[slot, span])
    copies.finish()


def settle_kernel(r_ref, scol_ref, out_ref):
    out_ref[...] = dot(one_hot_cols(scol_ref[:, 0:1], r_ref.shape[0]), r_ref[...]).astype(BF)


def shape(dims, kind):
    return jax.ShapeDtypeStruct(dims, kind)


marks = {}


def call(kernel, ins, outs, scratch=(), deps=(), us=1.0, scalars=0, ins_any=0, outs_any=0, limit=24, aliases=None):
    n_in, n_out = len(ins), len(outs)
    whole = pl.BlockSpec(memory_space=pl.ANY)
    held = pl.BlockSpec(memory_space=pltpu.HBM)
    before = [marks.get(id(d), (d, d))[1] for d in deps]

    def body(*refs):
        skip = n_in + len(before)
        kernel(*refs[:n_in], *refs[skip : skip + n_out], *refs[skip + n_out + 1 :])

    made = pl.pallas_call(
        body,
        out_shape=[*outs, shape((8, LANES), F32)],
        in_specs=[smem()] * scalars + vmem(n_in - scalars - ins_any) + [whole] * (ins_any - len(aliases or ())) + [held] * len(aliases or ()) + [whole] * len(before),
        out_specs=vmem(n_out - outs_any) + [held] * (outs_any + 1),
        scratch_shapes=list(scratch),
        input_output_aliases=aliases or {},
        compiler_params=params(limit << 20),
        cost_estimate=cost(1e9 * us, 0),
    )(*ins, *before)
    for out in made[:-1]:
        marks[id(out)] = (out, made[-1])
    return made[:-1]


def per_device(
    block_input, cotangent, source, seq_lengths, qkv_weight, qv_bias, out_weight, out_bias,
    up_weight, up_bias, down_weight, down_bias, rezero_alphas,
):
    marks.clear()
    micros, rows, width = block_input.shape
    groups = lax.axis_size("dp")
    tensors = lax.axis_size("tensor")
    lanes = qkv_weight.shape[2]
    units = up_weight.shape[1]
    blocks = min(groups, 8)
    me, tensor = lax.axis_index("dp"), lax.axis_index("tensor")
    ids = jnp.stack([me, tensor]).astype(I32)
    lengths = lax.dynamic_index_in_dim(seq_lengths, tensor, 0, keepdims=False)[0]

    def across(axis, bit, value):
        count = tensors if axis == "tensor" else groups
        return lax.ppermute(value, axis, [(i, i ^ bit) for i in range(count)])

    def after(value, *others):
        return lax.optimization_barrier((value, *others))[0] if others else value

    def by_micro(kernel, n_whole, out_shape, scratch):
        return pl.pallas_call(
            kernel,
            out_shape=out_shape,
            grid_spec=pltpu.PrefetchScalarGridSpec(
                num_scalar_prefetch=1,
                grid=(1,),
                in_specs=[
                    pl.BlockSpec(source.shape, lambda i, s: (0, 0)),
                    pl.BlockSpec((1, rows, width), lambda i, s: (s[1], 0, 0)),
                ]
                + [pl.BlockSpec((rows // LANES, LANES), lambda i, s: (0, 0))] * n_whole,
                out_specs=[pl.BlockSpec(o.shape, lambda i, s: (0, 0)) for o in out_shape],
                scratch_shapes=scratch,
            ),
            compiler_params=params(),
            cost_estimate=cost(1e9 * C["route"], 0),
        )

    hot = pltpu.VMEM((rows, rows), BF)
    xs, srow, scol = by_micro(
        functools.partial(route_kernel, groups), 0,
        [shape((rows, width), BF), shape((rows // LANES, LANES), I32), shape((rows, LANES), I32)], [hot],
    )(ids, source, block_input)

    def exchange(rows_out):
        return lax.all_to_all(rows_out.reshape(groups, rows // groups, width), "dp", 0, 0, tiled=True).reshape(rows, width)

    arr_x = exchange(xs)
    gs, arow, acol = by_micro(
        second_kernel, 1,
        [shape((rows, width), BF), shape((8, rows), I32), shape((rows, LANES), I32)], [hot],
    )(ids, source, cotangent, srow)
    head = jnp.concatenate([qv_bias, up_bias.reshape(units // lanes, lanes), jnp.zeros((2, lanes), BF)], axis=0)
    own = (head, qkv_weight, out_weight, up_weight, down_weight)
    far = [across("tensor", 2, w) for w in own]
    held = lax.optimization_barrier((*far[:3], arow))[:3]

    def four(own, far):
        return own, across("tensor", 1, own), far, across("tensor", 1, far)

    bias4, wa4, wo4 = [four(w, f) for w, f in zip(own, held)]
    arr_g = exchange(gs)

    def v16(*dims):
        return pltpu.VMEM(dims, BF)

    def v32(*dims):
        return pltpu.VMEM(dims, F32)

    def sems(count):
        return pltpu.SemaphoreType.DMA((count,))

    ff = tensors * units
    wide = [shape((rows, width), BF)] * 4
    logs, x, q, k, v, o, h, low, attn = call(
        attend_kernel,
        (ids, lengths, rezero_alphas, *bias4, out_bias.reshape(1, width), acol, arr_x, *wa4, *wo4),
        [shape((2 * tensors, rows), F32), *wide, shape((rows, width), BF), shape((rows, width), F32),
         shape((rows, width), BF), shape((rows, width), F32)],
        [sems(40), v16(rows, width), v16(width, 3 * width), v16(width, width), v32(8, width), hot, v16(rows, width),
         v16(rows, width), v16(rows, width), v16(rows, width), v16(rows, width), v32(rows, width),
         v16(rows, width), v32(rows, width)],
        scalars=3, ins_any=9, outs_any=8, us=C["attend"], limit=60,
    )
    held = lax.optimization_barrier((*far[3:], logs))[:2]
    wu4, wd4 = [four(w, f) for w, f in zip(own[3:], held)]
    ys, act, slope, branch = call(
        forward_kernel,
        (rezero_alphas, *bias4, down_bias.reshape(1, width), arow, low, h, *wu4, *wd4),
        [shape((rows, width), BF), shape((rows, ff), BF), shape((rows, ff), F32), shape((rows, width), F32)],
        [sems(40), v16(rows, width), v32(rows, width), v16(width, ff), v16(ff, width), v16(rows, ff), v32(rows, ff),
         v32(rows, width), v16(rows, width), hot, v16(rows, width)],
        scalars=1, ins_any=10, outs_any=4, us=C["forward"], limit=60,
    )
    bundle = (width + units + lanes) // blocks
    part = shape((tensors // 2, blocks, bundle, width), BF)
    small1, go, gh, keep1, send1 = call(
        feed_kernel,
        (ids, rezero_alphas, acol, arr_g, *wu4, *wd4, *wo4, act, slope, low, branch, attn, o),
        [shape((8, width), F32), shape((rows, width), BF), shape((rows, width), F32),
         shape(part.shape, F32), part],
        [sems(48), v16(rows, width), v16(width, ff), v16(ff, width), v16(width, width), v16(rows, ff), v32(rows, ff),
         v16(rows, width), v32(rows, width), v32(rows, width), v16(rows, width),
         hot, v16(rows, width), v16(rows, width), v16(rows, ff), v32(rows, width), v16(rows, width), v16(rows, width),
         v32(*part.shape), v16(*part.shape), v32(width, width)],
        scalars=2, ins_any=19, outs_any=4, us=C["feed"], deps=(ys,), limit=60,
    )
    arr_y = exchange(ys)
    got = across("tensor", 1, send1)

    def back(first, last, deps):
        span = (last - first) * lanes
        return call(
            functools.partial(back_kernel, first), (lengths, logs, q, k, v, go),
            [shape((3, rows, span), BF)],
            [sems(16), v16(rows, span), v16(rows, span), v16(rows, span), v16(rows, span), v16(3, rows, span), v32(rows, lanes), v32(rows, lanes)],
            scalars=1, ins_any=4, outs_any=1, limit=60, deps=deps, us=C["back"],
        )[0]

    half = tensors // 2
    bare = shape((16, width), F32)

    def blocks_of(n, like, kind):
        return shape((n, *like.shape[1:]), kind)

    def settle(rows_back, deps):
        return call(settle_kernel, (rows_back, scol), [shape((rows, width), BF)], deps=deps, us=C["settle"])[0]

    def widen(first, a, b, into=None, deps=()):
        extra = () if into is None else (into,)
        return call(
            functools.partial(widen_kernel, first), (ids, a, b, *extra), [shape((tensors, rows, width), F32)],
            [sems(8), v32(2, rows, width), v16(2, rows, width)],
            scalars=1, ins_any=2 + len(extra), outs_any=1, us=C["widen"], deps=deps, aliases={3: 0} if extra else None,
        )[0]

    def relay(value, deps):
        return call(lambda *refs: None, (value,), [shape(value.shape, value.dtype)], ins_any=1, outs_any=1, aliases={0: 0}, deps=deps, us=0.1)[0]

    def gather(own):
        y0, r4, r2 = across("dp", 1, own), across("dp", 4, own), across("dp", 2, own)
        r4 = relay(r4, (y0, r2))
        y4, r6 = across("dp", 1, r4), across("dp", 2, r4)
        r2 = relay(r2, (y4, r6))
        return [own, y0, r2, across("dp", 1, r2), r4, y4, r6, across("dp", 1, r6)]

    keep1 = keep1.reshape(half * blocks, bundle, width)
    send1 = send1.reshape(half * blocks, bundle, width)
    got = across("tensor", 1, send1)
    n = half * blocks // 2
    even, low_half = (lambda b: b % 2 == 0), (lambda b: b < blocks // 2)
    keep1, send1 = call(
        functools.partial(halve_kernel, even), (keep1, got), [blocks_of(n, keep1, F32), blocks_of(n, keep1, BF)], us=C["halve"]
    )
    got_y = across("dp", 1, send1)
    grad_a = back(0, half, (keep1,))
    grad_b = back(half, tensors, (grad_a,))
    y_own = settle(arr_y, (grad_b,))
    y_far = across("tensor", 2, y_own)
    y_core = across("tensor", 1, y_own)
    n = n // 2
    keep1, send1 = call(
        functools.partial(halve_kernel, low_half), (keep1, got_y), [blocks_of(n, keep1, F32), blocks_of(n, keep1, BF)],
        deps=(y_own,), us=C["halve"],
    )
    got_x = across("tensor", 2, send1)
    share = (3 * width) // blocks
    split = 2 * 16 * width // LANES
    n2 = half * blocks
    small, keep2, send2 = call(
        weight_kernel, (ids, small1, grad_a, grad_b, x),
        [bare, shape((n2, share, lanes), F32), shape((n2 + 1, share, lanes), BF)],
        [sems(20), v16(rows, 3 * width), v16(rows, width), v32(n2, share, lanes), v16(n2, share, lanes), v32(width, 3 * width),
         v16(split, LANES)],
        scalars=1, ins_any=3, outs_any=2, us=C["weight"], deps=(keep1,), limit=60,
    )
    gxs = call(
        last_kernel, (ids, arow, grad_a, grad_b, gh, *wa4), [shape((rows, width), BF)],
        [sems(40), v16(rows, 3 * width), v32(rows, width), v16(width, 3 * width), hot, v16(rows, width), v16(rows, width)],
        scalars=1, ins_any=7, outs_any=1, us=C["last"], deps=(small,), limit=60,
    )[0]
    arr_gx = exchange(gxs)
    got = across("tensor", 1, send2)
    n2 = n2 // 2
    keep2, small, send2 = call(
        functools.partial(halve_small_kernel, lambda b: b < blocks), (keep2, small, got),
        [blocks_of(n2, keep2, F32), bare, blocks_of(n2 + 1, keep2, BF)], deps=(gxs,), us=C["part"],
    )
    got = across("tensor", 2, send2)
    own1, *parts1 = call(
        part_kernel, (keep1, got_x), [shape(keep1.shape[1:], F32)] + [shape(keep1.shape[1:], BF)] * (blocks // 2 - 1),
        deps=(keep2, y_far), us=C["part"],
    )
    got1 = [across("dp", 2 * (j + 1), v) for j, v in enumerate(parts1)]
    y_late = call(lambda *refs: None, (y_far,), [shape((rows, width), BF)], ins_any=1, outs_any=1, aliases={0: 0}, deps=(own1,), us=0.1)[0]
    output = widen(0, y_own, y_core, deps=(own1,))
    shared, small = call(
        whole_small_kernel, (keep2, small, got), [shape((blocks, share + split, lanes), BF), bare], deps=(output,), us=C["part"],
    )
    ranks = None if groups == blocks else [list(range(g, g + blocks)) for g in range(0, groups, blocks)]
    shared = lax.all_to_all(shared, "dp", 0, 0, tiled=True, axis_index_groups=ranks)
    gx_own = settle(arr_gx, (small, y_late))
    gx_far = across("tensor", 2, gx_own)
    gx_core = across("tensor", 1, gx_own)
    y_both = across("tensor", 1, y_late)
    own1 = call(sum_kernel, (own1, *got1), [shape(own1.shape, F32)], deps=(gx_own,), us=C["part"])[0]
    output = widen(2, y_late, y_both, output, deps=(own1,))
    gx_grad = widen(0, gx_own, gx_core, deps=(output,))
    kind = BF if groups <= blocks else F32
    own, small = call(
        pack_kernel, (own1, shared), [shape((bundle + share // 4, width), kind), bare], deps=(gx_grad,), us=C["halve"]
    )
    bit = blocks
    while bit < groups:
        kind = BF if 2 * bit == groups else F32
        own, small = call(
            add_one_kernel, (own, across("dp", bit, own), small, across("dp", bit, small)), [shape(own.shape, kind), bare]
        )
        bit *= 2
    gathered = gather(own)
    gx_far = relay(gx_far, (gathered[blocks - 2],))
    gx_both = across("tensor", 1, gx_far)
    qkv_grad, qv_grad, out_grad, ob_grad, up_grad, ub_grad, down_grad, db_grad, alphas = call(
        functools.partial(spread_kernel, blocks), (ids, small, *gathered),
        [shape((3, width, lanes), F32), shape((2, lanes), F32), shape((lanes, width), F32), shape((1, width), F32),
         shape((width, units), F32), shape((1, units), F32), shape((units, width), F32), shape((1, width), F32), shape((8, LANES), F32)],
        [v32(width, units), v32(share, lanes)], scalars=1, us=C["spread"],
    )
    input_grad = widen(2, gx_far, gx_both, gx_grad, deps=())
    return (
        output, input_grad, qkv_grad, qv_grad, out_grad, ob_grad[0], up_grad, ub_grad[0], down_grad, db_grad[0], alphas[0:2, 0],
    )


def solution(mesh):
    in_specs = (
        P(None, "dp", None), P(None, "dp", None), P(), P(None, "dp", None),
        P(None, None, "tensor"), P(None, "tensor"), P("tensor", None), P(),
        P(None, "tensor"), P("tensor"), P("tensor", None), P(), P(),
    )
    out_specs = (
        P(None, "dp", None), P(None, "dp", None), P(None, None, "tensor"), P(None, "tensor"),
        P("tensor", None), P(), P(None, "tensor"), P("tensor"), P("tensor", None), P(), P(),
    )
    return jax.shard_map(per_device, mesh=mesh, in_specs=in_specs, out_specs=out_specs, check_vma=False)
```

profile of v0, /device:TPU:0, one launch (start us, length us, event | category | flops | bytes accessed | tf_op | source)
XLA Modules:
  0.0 276.6 jit_solution(16784607871696719800)
XLA Ops:
  1.3 6.2 %shard_map.212 = (bf16[1024,512]{1,0:T(8,128)(2,1)}, s32[8,128]{1,0:T(8,128)}, s32[1024,128]{1,0:T(8,128)}) custom-call(s32[2]{0:T(128)} %pad_add_fusion.ids_ref.refs_0_, s32[4,8192]{1,0:T(4,128)} %src_ref.3, bf16[4,1024,512]{2,1,0:T(8,128)(2,1)} %x_ref.1), custom_call_target="tpu_custom_call" | custom-call | flops 6000000000 | tf_op jit(solution)/shard_map/pallas_call | solution.py:737
  7.6 7.3 %all-to-all-start = ((bf16[8,128,512]{2,1,0:T(8,128)(2,1)}), bf16[8,128,512]{2,1,0:T(8,128)(2,1)S(1)}, u32[]{:S(2)}, u32[]{:S(2)}) async-start(bf16[8,128,512]{2,1,0:T(8,128)(2,1)} %bitcast.21), calls=%async_computation | async-start | bytes 2097152 | tf_op jit(solution)/shard_map/all_to_all | solution.py:743
  18.7 4.8 %shard_map.213 = (bf16[1024,512]{1,0:T(8,128)(2,1)}, s32[8,1024]{1,0:T(8,128)}, s32[1024,128]{1,0:T(8,128)}) custom-call(s32[2]{0:T(128)} %pad_add_fusion.ids_ref.refs_0_, s32[4,8192]{1,0:T(4,128)} %src_ref.3, bf16[4,1024,512]{2,1,0:T(8,128)(2,1)} %g_ref.1, s32[8,128]{1,0:T(8,128)} %get-tuple-element.97.srow_ref), custom_call_target="tpu_custom_call" | custom-call | flops 6000000000 | tf_op jit(solution)/shard_map/pallas_call | solution.py:746
  23.6 3.5 %collective-permute-done.1.refs_5_.refs_3_ = bf16[8,128]{1,0:T(8,128)(2,1)S(1)} collective-permute-done((bf16[8,128]{1,0:T(8,128)(2,1)S(1)}, bf16[8,128]{1,0:T(8,128)(2,1)S(1)}, u32[]{:S(2)}, u32[]{:S(2)}) %collective-permute-start.1) | collective-permute-done | bytes 2080 | tf_op jit(solution)/shard_map/ppermute | solution.py:712
  35.6 5.1 %all-to-all-done = bf16[8,128,512]{2,1,0:T(8,128)(2,1)S(1)} async-done(((bf16[8,128,512]{2,1,0:T(8,128)(2,1)}), bf16[8,128,512]{2,1,0:T(8,128)(2,1)S(1)}, u32[]{:S(2)}, u32[]{:S(2)}) %all-to-all-start) | async-done | bytes 1048608 | tf_op jit(solution)/shard_map/all_to_all | solution.py:743
  40.7 3.9 %all-to-all-start.2 = ((bf16[8,128,512]{2,1,0:T(8,128)(2,1)}), bf16[8,128,512]{2,1,0:T(8,128)(2,1)S(1)}, u32[]{:S(2)}, u32[]{:S(2)}) async-start(bf16[8,128,512]{2,1,0:T(8,128)(2,1)} %bitcast.19), calls=%async_computation.2 | async-start | bytes 2097152 | tf_op jit(solution)/shard_map/all_to_all | solution.py:743
  44.6 18.6 %shard_map.214 = (f32[8,1024]{1,0:T(8,128)}, bf16[1024,512]{1,0:T(8,128)(2,1)}, bf16[1024,512]{1,0:T(8,128)(2,1)}, bf16[1024,512]{1,0:T(8,128)(2,1)}, bf16[1024,...) custom-call(s32[2]{0:T(128)} %pad_add_fusion.ids_ref.refs_0_, ...), custom_call_target="tpu_custom_call" | custom-call | flops 19000000512 | tf_op jit(solution)/shard_map/pallas_call | solution.py:680
  67.0 15.4 %shard_map.215 = (bf16[1024,512]{1,0:T(8,128)(2,1)}, bf16[1024,2048]{1,0:T(8,128)(2,1)}, f32[1024,2048]{1,0:T(8,128)}, f32[1024,512]{1,0:T(8,128)}, f32[8,128]{1,0:T(8,128)}) custom-call(f32[2]{0:T(128)} %refs_1_.1, bf16[8,128]{1,0:T(8,128)(2,1)} %copy-done.20, bf16[8,128]{1,0:T(8,128)(2,1)} %copy-done.36, bf16[8,128]{1,0:T(8,128)(2,1)} %copy-done.35, ...), custom_call_target="tpu_custom_call" | custom-call | flops 5000000000 | tf_op jit(solution)/shard_map/pallas_call | solution.py:680
  83.4 18.7 %shard_map.216 = (f32[8,512]{1,0:T(8,128)}, bf16[1024,512]{1,0:T(8,128)(2,1)}, f32[1024,512]{1,0:T(8,128)}, f32[2,8,144,512]{3,2,1,0:T(8,128)}, bf16[2,8,144,512]{3,2,1,0:T(8,128)(2,1)}, /*index=5*/f32[8,128]{1,0:T(8,128)}) custom-call(s32[2]{0:T(128)} %pad_add_fusion.ids_ref.refs_0_, f32[2]{0:T(128)} %refs_1_.1, ...), custom_call_target="tpu_custom_call" | custom-call | flops 19000000512 | tf_op jit(solution)/shard_map/pallas_call | solution.py:680
  102.3 6.2 %all-to-all-start.1 = ((bf16[8,128,512]{2,1,0:T(8,128)(2,1)}), bf16[8,128,512]{2,1,0:T(8,128)(2,1)S(1)}, u32[]{:S(2)}, u32[]{:S(2)}) async-start(bf16[8,128,512]{2,1,0:T(8,128)(2,1)} %bitcast.24), calls=%async_computation.1 | async-start | bytes 2097152 | tf_op jit(solution)/shard_map/all_to_all | solution.py:743
  116.3 11.0 %shard_map.218 = (bf16[3,1024,256]{2,1,0:T(8,128)(2,1)}, f32[8,128]{1,0:T(8,128)}) custom-call(s32[3]{0:T(128)} %dynamic-slice_reduce_fusion.refs_1_.refs_0_, f32[8,1024]{1,0:T(8,128)} %get-tuple-element.106.refs_1_, bf16[1024,512]{1,0:T(8,128)(2,1)} %get-tuple-element.111.refs_2_, bf16[1024,512]{1,0:T(8,128)(2,1)} %get-tuple-element.112.refs_3_, ...), custom_call_target="tpu_custom_call" | custom-call | flops 11000000512 | tf_op jit(solution)/shard_map/pallas_call | solution.py:680
  127.4 11.5 %shard_map.219 = (bf16[3,1024,256]{2,1,0:T(8,128)(2,1)}, f32[8,128]{1,0:T(8,128)}) custom-call(s32[3]{0:T(128)} %dynamic-slice_reduce_fusion.refs_1_.refs_0_, f32[8,1024]{1,0:T(8,128)} %get-tuple-element.106.refs_1_, bf16[1024,512]{1,0:T(8,128)(2,1)} %get-tuple-element.111.refs_2_, bf16[1024,512]{1,0:T(8,128)(2,1)} %get-tuple-element.112.refs_3_, ...), custom_call_target="tpu_custom_call" | custom-call | flops 11000000512 | tf_op jit(solution)/shard_map/pallas_call | solution.py:680
  143.5 5.1 %collective-permute-done.17.refs_1_ = bf16[8,144,512]{2,1,0:T(8,128)(2,1)} collective-permute-done((bf16[8,144,512]{2,1,0:T(8,128)(2,1)}, bf16[8,144,512]{2,1,0:T(8,128)(2,1)}, u32[]{:S(2)}, u32[]{:S(2)}) %collective-permute-start.17) | collective-permute-done | bytes 1179680 | tf_op jit(solution)/shard_map/ppermute | solution.py:712
  154.1 6.7 %shard_map.222 = (f32[16,512]{1,0:T(8,128)}, f32[16,192,128]{2,1,0:T(8,128)}, bf16[17,192,128]{2,1,0:T(8,128)(2,1)}, f32[8,128]{1,0:T(8,128)}) custom-call(s32[2]{0:T(128)} %pad_add_fusion.ids_ref.refs_0_, f32[8,512]{1,0:T(8,128)} %get-tuple-element.133.refs_1_, bf16[3,1024,256]{2,1,0:T(8,128)(2,1)} %get-tuple-element.134.refs_2_, ...), custom_call_target="tpu_custom_call" | custom-call | flops 200000000 | tf_op jit(solution)/shard_map/pallas_call | solution.py:680
  160.9 7.9 %shard_map.223 = (bf16[1024,512]{1,0:T(8,128)(2,1)}, f32[8,128]{1,0:T(8,128)}) custom-call(s32[2]{0:T(128)} %pad_add_fusion.ids_ref.refs_0_, s32[8,1024]{1,0:T(8,128)} %get-tuple-element.98.refs_6_.refs_1_, bf16[3,1024,256]{2,1,0:T(8,128)(2,1)} %get-tuple-element.134.refs_2_, bf16[3,1024,256]{2,1,0:T(8,128)(2,1)} %get-tuple-element.135.refs_3_, ...), custom_call_target="tpu_custom_call" | custom-call | flops 20000000000 | tf_op jit(solution)/shard_map/pallas_call | solution.py:680
  168.7 6.2 %all-to-all-start.3 = ((bf16[8,128,512]{2,1,0:T(8,128)(2,1)}), bf16[8,128,512]{2,1,0:T(8,128)(2,1)S(1)}, u32[]{:S(2)}, u32[]{:S(2)}) async-start(bf16[8,128,512]{2,1,0:T(8,128)(2,1)} %bitcast.22), calls=%async_computation.3 | async-start | bytes 2097152 | tf_op jit(solution)/shard_map/all_to_all | solution.py:743
  178.0 2.5 collective-permute-done.18.refs_1_
  187.9 3.9 %shard_map.227 = (f32[4,1024,512]{2,1,0:T(8,128)}, f32[8,128]{1,0:T(8,128)S(1)}) custom-call(s32[2]{0:T(128)S(1)} %copy-done.4, bf16[1024,512]{1,0:T(8,128)(2,1)} %get-tuple-element.127.refs_1_, bf16[1024,512]{1,0:T(8,128)(2,1)} %collective-permute-done.21.refs_2_, f32[8,128]{1,0:T(8,128)S(1)} %get-tuple-element.145.refs_1_.refs_3_), custom_call_target="tpu_custom_call" | custom-call | flops 5000000000 | tf_op jit(solution)/shard_map/pallas_call | solution.py:680
  191.8 5.5 %collective-permute-done.25.refs_2_ = bf16[9,192,128]{2,1,0:T(8,128)(2,1)S(1)} collective-permute-done((bf16[9,192,128]{2,1,0:T(8,128)(2,1)S(1)}, bf16[9,192,128]{2,1,0:T(8,128)(2,1)S(1)}, u32[]{:S(2)}, u32[]{:S(2)}) %collective-permute-start.25) | collective-permute-done | bytes 442400 | tf_op jit(solution)/shard_map/ppermute | solution.py:712
  198.3 10.1 %all-to-all-done.3 = bf16[8,128,512]{2,1,0:T(8,128)(2,1)S(1)} async-done(((bf16[8,128,512]{2,1,0:T(8,128)(2,1)}), bf16[8,128,512]{2,1,0:T(8,128)(2,1)S(1)}, u32[]{:S(2)}, u32[]{:S(2)}) %all-to-all-start.3) | async-done | bytes 1048608 | tf_op jit(solution)/shard_map/all_to_all | solution.py:743
  211.7 3.5 %all-to-all-start.4 = ((bf16[8,320,128]{2,1,0:T(8,128)(2,1)}), bf16[8,320,128]{2,1,0:T(8,128)(2,1)S(1)}, u32[]{:S(2)}, u32[]{:S(2)}) async-start(bf16[8,320,128]{2,1,0:T(8,128)(2,1)} %get-tuple-element.164), calls=%async_computation.4 | async-start | bytes 1310720 | tf_op jit(solution)/shard_map/all_to_all | solution.py:898
  216.9 3.9 %shard_map.231 = (f32[4,1024,512]{2,1,0:T(8,128)}, f32[8,128]{1,0:T(8,128)S(1)}) custom-call(s32[2]{0:T(128)S(1)} %copy-done.4, bf16[1024,512]{1,0:T(8,128)(2,1)S(1)} %get-tuple-element.146.refs_1_, bf16[1024,512]{1,0:T(8,128)(2,1)} %collective-permute-done.20.refs_2_, f32[4,1024,512]{2,1,0:T(8,128)} %get-tuple-element.147.refs_3_, ...), custom_call_target="tpu_custom_call", output_to_operand_aliasing={{0}: (3, {})} | custom-call | flops 5000000000 | tf_op jit(solution)/shard_map/pallas_call | solution.py:680
  220.8 3.9 %shard_map.232 = (f32[4,1024,512]{2,1,0:T(8,128)}, f32[8,128]{1,0:T(8,128)S(1)}) custom-call(s32[2]{0:T(128)S(1)} %copy-done.4, bf16[1024,512]{1,0:T(8,128)(2,1)} %get-tuple-element.162.refs_1_, bf16[1024,512]{1,0:T(8,128)(2,1)} %collective-permute-done.27.refs_2_, f32[8,128]{1,0:T(8,128)S(1)} %get-tuple-element.165.refs_3_), custom_call_target="tpu_custom_call" | custom-call | flops 5000000000 | tf_op jit(solution)/shard_map/pallas_call | solution.py:680
  224.7 8.7 %all-to-all-done.4.refs_1_ = bf16[8,320,128]{2,1,0:T(8,128)(2,1)S(1)} async-done(((bf16[8,320,128]{2,1,0:T(8,128)(2,1)}), bf16[8,320,128]{2,1,0:T(8,128)(2,1)S(1)}, u32[]{:S(2)}, u32[]{:S(2)}) %all-to-all-start.4) | async-done | bytes 655392 | tf_op jit(solution)/shard_map/all_to_all | solution.py:898
  237.1 5.5 %collective-permute-done.30.refs_2_.refs_0_ = bf16[192,512]{1,0:T(8,128)(2,1)S(1)} collective-permute-done((bf16[192,512]{1,0:T(8,128)(2,1)S(1)}, bf16[192,512]{1,0:T(8,128)(2,1)S(1)}, u32[]{:S(2)}, u32[]{:S(2)}) %collective-permute-start.30) | collective-permute-done | bytes 196640 | tf_op jit(solution)/shard_map/ppermute | solution.py:712
  242.7 3.9 %collective-permute-done.28.refs_0_ = bf16[192,512]{1,0:T(8,128)(2,1)S(1)} collective-permute-done((bf16[192,512]{1,0:T(8,128)(2,1)S(1)}, bf16[192,512]{1,0:T(8,128)(2,1)S(1)}, u32[]{:S(2)}, u32[]{:S(2)}) %collective-permute-start.28) | collective-permute-done | bytes 196640 | tf_op jit(solution)/shard_map/ppermute | solution.py:712
  246.6 5.7 %collective-permute-done.31.refs_1_.refs_2_.refs_8_ = bf16[192,512]{1,0:T(8,128)(2,1)S(1)} collective-permute-done((bf16[192,512]{1,0:T(8,128)(2,1)S(1)}, bf16[192,512]{1,0:T(8,128)(2,1)S(1)}, u32[]{:S(2)}, u32[]{:S(2)}) %collective-permute-start.31) | collective-permute-done | bytes 196640 | tf_op jit(solution)/shard_map/ppermute | solution.py:712
  252.8 6.7 %collective-permute-done.33.refs_1_.refs_7_ = bf16[192,512]{1,0:T(8,128)(2,1)S(1)} collective-permute-done((bf16[192,512]{1,0:T(8,128)(2,1)S(1)}, bf16[192,512]{1,0:T(8,128)(2,1)S(1)}, u32[]{:S(2)}, u32[]{:S(2)}) %collective-permute-start.33) | collective-permute-done | bytes 196640 | tf_op jit(solution)/shard_map/ppermute | solution.py:712
  261.6 5.8 %collective-permute-done.34.refs_5_ = bf16[192,512]{1,0:T(8,128)(2,1)S(1)} collective-permute-done((bf16[192,512]{1,0:T(8,128)(2,1)S(1)}, bf16[192,512]{1,0:T(8,128)(2,1)S(1)}, u32[]{:S(2)}, u32[]{:S(2)}) %collective-permute-start.34) | collective-permute-done | bytes 196640 | tf_op jit(solution)/shard_map/ppermute | solution.py:712
  267.3 2.9 %collective-permute-done.35.refs_9_ = bf16[192,512]{1,0:T(8,128)(2,1)S(1)} collective-permute-done((bf16[192,512]{1,0:T(8,128)(2,1)S(1)}, bf16[192,512]{1,0:T(8,128)(2,1)S(1)}, u32[]{:S(2)}, u32[]{:S(2)}) %collective-permute-start.35) | collective-permute-done | bytes 196640 | tf_op jit(solution)/shard_map/ppermute | solution.py:712
  270.3 2.6 shard_map.238
  273.5 2.8 %shard_map.236 = (f32[4,1024,512]{2,1,0:T(8,128)}, f32[8,128]{1,0:T(8,128)}) custom-call(s32[2]{0:T(128)S(1)} %copy-done.4, bf16[1024,512]{1,0:T(8,128)(2,1)S(1)} %get-tuple-element.169.refs_1_, bf16[1024,512]{1,0:T(8,128)(2,1)S(1)} %collective-permute-done.32.refs_2_, f32[4,1024,512]{2,1,0:T(8,128)} %get-tuple-element.170.refs_3_), custom_call_target="tpu_custom_call", output_to_operand_aliasing={{0}: (3, {})} | custom-call | flops 5000000000 | tf_op jit(solution)/shard_map/pallas_call | solution.py:680
  (161 shorter events, 59.1 us)
Async XLA Ops:
  7.6 33.1 %all-to-all-start = ((bf16[8,128,512]{2,1,0:T(8,128)(2,1)}), bf16[8,128,512]{2,1,0:T(8,128)(2,1)S(1)}, u32[]{:S(2)}, u32[]{:S(2)}) async-start(bf16[8,128,512]{2,1,0:T(8,128)(2,1)} %bitcast.21), calls=%async_computation | async-start | bytes 2097152 | tf_op jit(solution)/shard_map/all_to_all | solution.py:743
  14.9 19.6 %collective-permute-start.5 = (bf16[3,512,128]{2,1,0:T(8,128)(2,1)S(1)}, bf16[3,512,128]{2,1,0:T(8,128)(2,1)S(1)}, u32[]{:S(2)}, u32[]{:S(2)}) collective-permute-start(bf16[3,512,128]{2,1,0:T(8,128)(2,1)S(1)} %copy-done.29), channel_id=1, source_target_pairs={{0,1},{1,0},{2,3},{3,2},{4,5},{5,4},{6,7},{7,6},{8,9},{9,8},{10,11... | collective-permute-start | bytes 1179656 | tf_op jit(solution)/shard_map/ppermute | solution.py:712
  15.0 14.4 %collective-permute-start.2 = (bf16[3,512,128]{2,1,0:T(8,128)(2,1)S(1)}, bf16[3,512,128]{2,1,0:T(8,128)(2,1)}, u32[]{:S(2)}, u32[]{:S(2)}) collective-permute-start(bf16[3,512,128]{2,1,0:T(8,128)(2,1)S(1)} %copy-done.29), channel_id=1, source_target_pairs={{0,2},{1,3},{2,0},{3,1},{4,6},{5,7},{6,4},{7,5},{8,10},{9,11},{10,... | collective-permute-start | bytes 1179656 | tf_op jit(solution)/shard_map/ppermute | solution.py:712
  16.7 10.4 %collective-permute-start.1 = (bf16[8,128]{1,0:T(8,128)(2,1)S(1)}, bf16[8,128]{1,0:T(8,128)(2,1)S(1)}, u32[]{:S(2)}, u32[]{:S(2)}) collective-permute-start(bf16[8,128]{1,0:T(8,128)(2,1)S(1)} %maximum_maximum_fusion.refs_3_.refs_1_), channel_id=1, source_target_pairs={{0,2},{1,3},{2,0},{3,1},{4,6},{5,7},{6,4},{7,5},{8,10},{9,11},{10,... | collective-permute-start | bytes 6152 | tf_op jit(solution)/shard_map/ppermute | solution.py:712
  17.2 12.1 %collective-permute-start.3 = (bf16[128,512]{1,0:T(8,128)(2,1)S(1)}, bf16[128,512]{1,0:T(8,128)(2,1)S(1)}, u32[]{:S(2)}, u32[]{:S(2)}) collective-permute-start(bf16[128,512]{1,0:T(8,128)(2,1)S(1)} %copy-done.31), channel_id=1, source_target_pairs={{0,2},{1,3},{2,0},{3,1},{4,6},{5,7},{6,4},{7,5},{8,10},{9,11},{10,... | collective-permute-start | bytes 393224 | tf_op jit(solution)/shard_map/ppermute | solution.py:712
  29.3 15.2 %collective-permute-start.6 = (bf16[3,512,128]{2,1,0:T(8,128)(2,1)}, bf16[3,512,128]{2,1,0:T(8,128)(2,1)}, u32[]{:S(2)}, u32[]{:S(2)}) collective-permute-start(bf16[3,512,128]{2,1,0:T(8,128)(2,1)} %collective-permute-done.2.refs_12_.refs_7_), channel_id=1, source_target_pairs={{0,1},{1,0},{2,3},{3,2},{4,5},{5,4},{6,7},{7,6},{8,9},{9,8},{10,11... | collective-permute-start | bytes 1179656 | tf_op jit(solution)/shard_map/ppermute | solution.py:712
  32.9 30.3 %collective-permute-start.10 = (bf16[512,512]{1,0:T(8,128)(2,1)S(1)}, bf16[512,512]{1,0:T(8,128)(2,1)}, u32[]{:S(2)}, u32[]{:S(2)}) collective-permute-start(bf16[512,512]{1,0:T(8,128)(2,1)S(1)} %copy-done.25), channel_id=1, source_target_pairs={{0,2},{1,3},{2,0},{3,1},{4,6},{5,7},{6,4},{7,5},{8,10},{9,11},{10,... | collective-permute-start | bytes 1572872 | tf_op jit(solution)/shard_map/ppermute | solution.py:712
  34.5 30.0 %collective-permute-start.9 = (bf16[512,512]{1,0:T(8,128)(2,1)S(1)}, bf16[512,512]{1,0:T(8,128)(2,1)}, u32[]{:S(2)}, u32[]{:S(2)}) collective-permute-start(bf16[512,512]{1,0:T(8,128)(2,1)S(1)} %copy-done.25), channel_id=1, source_target_pairs={{0,1},{1,0},{2,3},{3,2},{4,5},{5,4},{6,7},{7,6},{8,9},{9,8},{10,11... | collective-permute-start | bytes 1572872 | tf_op jit(solution)/shard_map/ppermute | solution.py:712
  34.5 29.9 %collective-permute-start.13 = (bf16[512,512]{1,0:T(8,128)(2,1)S(1)}, bf16[512,512]{1,0:T(8,128)(2,1)}, u32[]{:S(2)}, u32[]{:S(2)}) collective-permute-start(bf16[512,512]{1,0:T(8,128)(2,1)S(1)} %copy-done.26), channel_id=1, source_target_pairs={{0,1},{1,0},{2,3},{3,2},{4,5},{5,4},{6,7},{7,6},{8,9},{9,8},{10,11... | collective-permute-start | bytes 1572872 | tf_op jit(solution)/shard_map/ppermute | solution.py:712
  35.0 28.2 %collective-permute-start.11 = (bf16[512,512]{1,0:T(8,128)(2,1)S(1)}, bf16[512,512]{1,0:T(8,128)(2,1)}, u32[]{:S(2)}, u32[]{:S(2)}) collective-permute-start(bf16[512,512]{1,0:T(8,128)(2,1)S(1)} %copy-done.26), channel_id=1, source_target_pairs={{0,2},{1,3},{2,0},{3,1},{4,6},{5,7},{6,4},{7,5},{8,10},{9,11},{10,... | collective-permute-start | bytes 1572872 | tf_op jit(solution)/shard_map/ppermute | solution.py:712
  40.7 41.7 %all-to-all-start.2 = ((bf16[8,128,512]{2,1,0:T(8,128)(2,1)}), bf16[8,128,512]{2,1,0:T(8,128)(2,1)S(1)}, u32[]{:S(2)}, u32[]{:S(2)}) async-start(bf16[8,128,512]{2,1,0:T(8,128)(2,1)} %bitcast.19), calls=%async_computation.2 | async-start | bytes 2097152 | tf_op jit(solution)/shard_map/all_to_all | solution.py:743
  102.3 36.6 %all-to-all-start.1 = ((bf16[8,128,512]{2,1,0:T(8,128)(2,1)}), bf16[8,128,512]{2,1,0:T(8,128)(2,1)S(1)}, u32[]{:S(2)}, u32[]{:S(2)}) async-start(bf16[8,128,512]{2,1,0:T(8,128)(2,1)} %bitcast.24), calls=%async_computation.1 | async-start | bytes 2097152 | tf_op jit(solution)/shard_map/all_to_all | solution.py:743
  114.3 34.4 %collective-permute-start.17 = (bf16[8,144,512]{2,1,0:T(8,128)(2,1)}, bf16[8,144,512]{2,1,0:T(8,128)(2,1)}, u32[]{:S(2)}, u32[]{:S(2)}) collective-permute-start(bf16[8,144,512]{2,1,0:T(8,128)(2,1)} %get-tuple-element.129), channel_id=1, source_target_pairs={{0,4},{4,0},{8,12},{12,8},{16,20},{20,16},{24,28},{28,24},{1,5},{5... | collective-permute-start | bytes 3538952 | tf_op jit(solution)/shard_map/ppermute | solution.py:712
  142.0 45.9 %collective-permute-start.21 = (bf16[1024,512]{1,0:T(8,128)(2,1)}, bf16[1024,512]{1,0:T(8,128)(2,1)}, u32[]{:S(2)}, u32[]{:S(2)}) collective-permute-start(bf16[1024,512]{1,0:T(8,128)(2,1)} %get-tuple-element.127.refs_1_), channel_id=1, source_target_pairs={{0,1},{1,0},{2,3},{3,2},{4,5},{5,4},{6,7},{7,6},{8,9},{9,8},{10,11... | collective-permute-start | bytes 3145736 | tf_op jit(solution)/shard_map/ppermute | solution.py:712
  142.0 35.9 %collective-permute-start.16 = (bf16[1024,512]{1,0:T(8,128)(2,1)}, bf16[1024,512]{1,0:T(8,128)(2,1)S(1)}, u32[]{:S(2)}, u32[]{:S(2)}) collective-permute-start(bf16[1024,512]{1,0:T(8,128)(2,1)} %get-tuple-element.127.refs_1_), channel_id=1, source_target_pairs={{0,2},{1,3},{2,0},{3,1},{4,6},{5,7},{6,4},{7,5},{8,10},{9,11},{10,... | collective-permute-start | bytes 3145736 | tf_op jit(solution)/shard_map/ppermute | solution.py:712
  152.6 27.9 %collective-permute-start.18 = (bf16[4,144,512]{2,1,0:T(8,128)(2,1)}, bf16[4,144,512]{2,1,0:T(8,128)(2,1)S(1)}, u32[]{:S(2)}, u32[]{:S(2)}) collective-permute-start(bf16[4,144,512]{2,1,0:T(8,128)(2,1)} %get-tuple-element.132), channel_id=1, source_target_pairs={{0,2},{1,3},{2,0},{3,1},{4,6},{5,7},{6,4},{7,5},{8,10},{9,11},{10,... | collective-permute-start | bytes 1769480 | tf_op jit(solution)/shard_map/ppermute | solution.py:712
  160.8 14.2 %collective-permute-start.19 = (bf16[17,192,128]{2,1,0:T(8,128)(2,1)}, bf16[17,192,128]{2,1,0:T(8,128)(2,1)S(1)}, u32[]{:S(2)}, u32[]{:S(2)}) collective-permute-start(bf16[17,192,128]{2,1,0:T(8,128)(2,1)} %get-tuple-element.140), channel_id=1, source_target_pairs={{0,1},{1,0},{2,3},{3,2},{4,5},{5,4},{6,7},{7,6},{8,9},{9,8},{10,11... | collective-permute-start | bytes 2506760 | tf_op jit(solution)/shard_map/ppermute | solution.py:712
  168.7 39.7 %all-to-all-start.3 = ((bf16[8,128,512]{2,1,0:T(8,128)(2,1)}), bf16[8,128,512]{2,1,0:T(8,128)(2,1)S(1)}, u32[]{:S(2)}, u32[]{:S(2)}) async-start(bf16[8,128,512]{2,1,0:T(8,128)(2,1)} %bitcast.22), calls=%async_computation.3 | async-start | bytes 2097152 | tf_op jit(solution)/shard_map/all_to_all | solution.py:743
  182.0 33.2 %collective-permute-start.22 = (bf16[144,512]{1,0:T(8,128)(2,1)}, bf16[144,512]{1,0:T(8,128)(2,1)S(1)}, u32[]{:S(2)}, u32[]{:S(2)}) collective-permute-start(bf16[144,512]{1,0:T(8,128)(2,1)} %get-tuple-element.149), channel_id=1, source_target_pairs={{0,8},{4,12},{8,0},{12,4},{16,24},{20,28},{24,16},{28,20},{1,9},{5... | collective-permute-start | bytes 442376 | tf_op jit(solution)/shard_map/ppermute | solution.py:712
  183.5 32.4 %collective-permute-start.23 = (bf16[144,512]{1,0:T(8,128)(2,1)}, bf16[144,512]{1,0:T(8,128)(2,1)S(1)}, u32[]{:S(2)}, u32[]{:S(2)}) collective-permute-start(bf16[144,512]{1,0:T(8,128)(2,1)} %get-tuple-element.150), channel_id=1, source_target_pairs={{0,16},{4,20},{8,24},{12,28},{16,0},{20,4},{24,8},{28,12},{1,17},{... | collective-permute-start | bytes 442376 | tf_op jit(solution)/shard_map/ppermute | solution.py:712
  185.9 30.0 %collective-permute-start.24 = (bf16[144,512]{1,0:T(8,128)(2,1)}, bf16[144,512]{1,0:T(8,128)(2,1)S(1)}, u32[]{:S(2)}, u32[]{:S(2)}) collective-permute-start(bf16[144,512]{1,0:T(8,128)(2,1)} %get-tuple-element.151), channel_id=1, source_target_pairs={{0,24},{4,28},{8,16},{12,20},{16,8},{20,12},{24,0},{28,4},{1,25},{... | collective-permute-start | bytes 442376 | tf_op jit(solution)/shard_map/ppermute | solution.py:712
  186.4 11.0 %collective-permute-start.25 = (bf16[9,192,128]{2,1,0:T(8,128)(2,1)S(1)}, bf16[9,192,128]{2,1,0:T(8,128)(2,1)S(1)}, u32[]{:S(2)}, u32[]{:S(2)}) collective-permute-start(bf16[9,192,128]{2,1,0:T(8,128)(2,1)S(1)} %get-tuple-element.155), channel_id=1, source_target_pairs={{0,2},{1,3},{2,0},{3,1},{4,6},{5,7},{6,4},{7,5},{8,10},{9,11},{10,... | collective-permute-start | bytes 1327112 | tf_op jit(solution)/shard_map/ppermute | solution.py:712
  187.9 29.0 %collective-permute-start.20 = (bf16[1024,512]{1,0:T(8,128)(2,1)S(1)}, bf16[1024,512]{1,0:T(8,128)(2,1)}, u32[]{:S(2)}, u32[]{:S(2)}) collective-permute-start(bf16[1024,512]{1,0:T(8,128)(2,1)S(1)} %get-tuple-element.146.refs_1_), channel_id=1, source_target_pairs={{0,1},{1,0},{2,3},{3,2},{4,5},{5,4},{6,7},{7,6},{8,9},{9,8},{10,11... | collective-permute-start | bytes 3145736 | tf_op jit(solution)/shard_map/ppermute | solution.py:712
  211.7 9.1 %collective-permute-start.27 = (bf16[1024,512]{1,0:T(8,128)(2,1)}, bf16[1024,512]{1,0:T(8,128)(2,1)}, u32[]{:S(2)}, u32[]{:S(2)}) collective-permute-start(bf16[1024,512]{1,0:T(8,128)(2,1)} %get-tuple-element.162.refs_1_), channel_id=1, source_target_pairs={{0,1},{1,0},{2,3},{3,2},{4,5},{5,4},{6,7},{7,6},{8,9},{9,8},{10,11... | collective-permute-start | bytes 3145736 | tf_op jit(solution)/shard_map/ppermute | solution.py:712
  211.7 21.8 %all-to-all-start.4 = ((bf16[8,320,128]{2,1,0:T(8,128)(2,1)}), bf16[8,320,128]{2,1,0:T(8,128)(2,1)S(1)}, u32[]{:S(2)}, u32[]{:S(2)}) async-start(bf16[8,320,128]{2,1,0:T(8,128)(2,1)} %get-tuple-element.164), calls=%async_computation.4 | async-start | bytes 1310720 | tf_op jit(solution)/shard_map/all_to_all | solution.py:898
  215.3 31.3 %collective-permute-start.26 = (bf16[1024,512]{1,0:T(8,128)(2,1)}, bf16[1024,512]{1,0:T(8,128)(2,1)S(1)}, u32[]{:S(2)}, u32[]{:S(2)}) collective-permute-start(bf16[1024,512]{1,0:T(8,128)(2,1)} %get-tuple-element.162.refs_1_), channel_id=1, source_target_pairs={{0,2},{1,3},{2,0},{3,1},{4,6},{5,7},{6,4},{7,5},{8,10},{9,11},{10,... | collective-permute-start | bytes 3145736 | tf_op jit(solution)/shard_map/ppermute | solution.py:712
  233.6 9.1 %collective-permute-start.30 = (bf16[192,512]{1,0:T(8,128)(2,1)S(1)}, bf16[192,512]{1,0:T(8,128)(2,1)S(1)}, u32[]{:S(2)}, u32[]{:S(2)}) collective-permute-start(bf16[192,512]{1,0:T(8,128)(2,1)S(1)} %get-tuple-element.167.refs_2_), channel_id=1, source_target_pairs={{0,8},{4,12},{8,0},{12,4},{16,24},{20,28},{24,16},{28,20},{1,9},{5... | collective-permute-start | bytes 589832 | tf_op jit(solution)/shard_map/ppermute | solution.py:712
  233.7 9.0 %collective-permute-start.29 = (bf16[192,512]{1,0:T(8,128)(2,1)S(1)}, bf16[192,512]{1,0:T(8,128)(2,1)S(1)}, u32[]{:S(2)}, u32[]{:S(2)}) collective-permute-start(bf16[192,512]{1,0:T(8,128)(2,1)S(1)} %get-tuple-element.167.refs_2_), channel_id=1, source_target_pairs={{0,4},{4,0},{8,12},{12,8},{16,20},{20,16},{24,28},{28,24},{1,5},{5... | collective-permute-start | bytes 589832 | tf_op jit(solution)/shard_map/ppermute | solution.py:712
  235.1 11.4 %collective-permute-start.28 = (bf16[192,512]{1,0:T(8,128)(2,1)S(1)}, bf16[192,512]{1,0:T(8,128)(2,1)S(1)}, u32[]{:S(2)}, u32[]{:S(2)}) collective-permute-start(bf16[192,512]{1,0:T(8,128)(2,1)S(1)} %get-tuple-element.167.refs_2_), channel_id=1, source_target_pairs={{0,16},{4,20},{8,24},{12,28},{16,0},{20,4},{24,8},{28,12},{1,17},{... | collective-permute-start | bytes 589832 | tf_op jit(solution)/shard_map/ppermute | solution.py:712
  252.2 21.3 %collective-permute-start.32 = (bf16[1024,512]{1,0:T(8,128)(2,1)S(1)}, bf16[1024,512]{1,0:T(8,128)(2,1)S(1)}, u32[]{:S(2)}, u32[]{:S(2)}) collective-permute-start(bf16[1024,512]{1,0:T(8,128)(2,1)S(1)} %get-tuple-element.169.refs_1_), channel_id=1, source_target_pairs={{0,1},{1,0},{2,3},{3,2},{4,5},{5,4},{6,7},{7,6},{8,9},{9,8},{10,11... | collective-permute-start | bytes 3145736 | tf_op jit(solution)/shard_map/ppermute | solution.py:712
  259.5 7.8 %collective-permute-start.34 = (bf16[192,512]{1,0:T(8,128)(2,1)S(1)}, bf16[192,512]{1,0:T(8,128)(2,1)S(1)}, u32[]{:S(2)}, u32[]{:S(2)}) collective-permute-start(bf16[192,512]{1,0:T(8,128)(2,1)S(1)} %get-tuple-element.173.refs_4_), channel_id=1, source_target_pairs={{0,4},{4,0},{8,12},{12,8},{16,20},{20,16},{24,28},{28,24},{1,5},{5... | collective-permute-start | bytes 589832 | tf_op jit(solution)/shard_map/ppermute | solution.py:712
  260.2 10.1 %collective-permute-start.35 = (bf16[192,512]{1,0:T(8,128)(2,1)S(1)}, bf16[192,512]{1,0:T(8,128)(2,1)S(1)}, u32[]{:S(2)}, u32[]{:S(2)}) collective-permute-start(bf16[192,512]{1,0:T(8,128)(2,1)S(1)} %collective-permute-done.31.refs_1_.refs_2_.refs_8_), channel_id=1, source_target_pairs={{0,4},{4,0},{8,12},{12,8},{16,20},{20,16},{24,28},{28,24},{1,5},{5... | collective-permute-start | bytes 589832 | tf_op jit(solution)/shard_map/ppermute | solution.py:712
  (47 other events, 329.4 us)
where the time goes:
time: 282 us; the launch traced here: 277 us
  Pallas kernels  128 us (45%)
  waiting for transfers between devices  76.2 us (27%)
  starting transfers between devices  53.1 us (19%)
  local copies, waits for them, and re-layouts  16.9 us (6%)
    pallas_call x25, Pallas kernels, call(): pl.pallas_call(body, out_shape=[*outs, shape((8, LANES), F32)], in_specs=...  117 us
    ppermute x36, waiting for transfers between devices, across(): return lax.ppermute(value, axis, [(i, i ^ bit) for i in range(count)])  52.3 us
    ppermute x36, starting transfers between devices, across(): return lax.ppermute(value, axis, [(i, i ^ bit) for i in range(count)])  25.9 us
    all_to_all x4, starting transfers between devices, exchange(): lax.all_to_all(rows_out.reshape(groups, rows // groups, width), 'dp', 0,...  23.6 us
    all_to_all x4, waiting for transfers between devices, exchange(): lax.all_to_all(rows_out.reshape(groups, rows // groups, width), 'dp', 0,...  15.1 us
    unnamed x76, local copies, waits for them, and re-layouts  14.3 us
    all_to_all x1, waiting for transfers between devices, per_device(): lax.all_to_all(shared, 'dp', 0, 0, tiled=True, axis_index_groups=ranks)  8.74 us
    pallas_call x1, Pallas kernels, per_device(): by_micro(functools.partial(route_kernel, groups), 0, [shape((rows, width)...  6.25 us
  transfers between devices with their start and end apart: 41, of which 17 were waited for; matrix products, arithmetic and copies ran while one was open for 1% of the time, Pallas kernels for 36%

commit v1 on v0

--- a/solution.py
+++ b/solution.py
@@ -10,7 +10,8 @@
 HEAD_SIZE = 64
 LANES = 128
 QT = 256
-FT = 512
+FT = 256
+SLAB = 16
 BF = jnp.bfloat16
 F32 = jnp.float32
 C = {"route": 6, "attend": 19, "forward": 5, "feed": 19, "back": 11, "halve": 1, "part": 5, "settle": 1, "last": 20, "weight": 0.2, "widen": 5, "spread": 3}
@@ -220,11 +221,24 @@
     copies.finish()
 
 
+def unit_biases(refs, units):
+    biases = []
+    for b in refs:
+        tail = b[...].astype(F32)
+        biases.append(jnp.concatenate([tail[2 + n : 3 + n, :] for n in range(units // LANES)], axis=1))
+    return biases
+
+
+def rise_of(z):
+    square = z * z
+    return 0.5 + 0.5 * jnp.tanh(z * (GELU_A + (GELU_A * GELU_B) * square)), square
+
+
 def forward_kernel(
     alpha_ref, b0_ref, b1_ref, b2_ref, b3_ref, db_ref, arow_ref,
     low_any, h_any, wu0_any, wu1_any, wu2_any, wu3_any, wd0_any, wd1_any, wd2_any, wd3_any,
-    ys_any, act_any, slope_any, f_any,
-    sems, low_ref, h_ref, wu_ref, wd_ref, act_ref, slope_ref, f_ref, y_ref, hot_ref, ys_ref,
+    ys_any, f_any,
+    sems, low_ref, h_ref, wu_ref, wd_ref, act_ref, f_ref, y_ref, hot_ref, ys_ref,
 ):
     rows, width = low_ref.shape
     units = wu0_any.shape[1]
@@ -236,10 +250,7 @@
     for j, wd in enumerate((wd0_any, wd1_any, wd2_any, wd3_any)):
         down.append(copies.start(wd, wd_ref.at[j * units : (j + 1) * units, :]))
     hidden = copies.start(h_any, h_ref)
-    biases = []
-    for b in (b0_ref, b1_ref, b2_ref, b3_ref):
-        tail = b[...].astype(F32)
-        biases.append(jnp.concatenate([tail[2 + n : 3 + n, :] for n in range(units // LANES)], axis=1))
+    biases = unit_biases((b0_ref, b1_ref, b2_ref, b3_ref), units)
     first.wait()
     items = [(j, m) for j in range(len(biases)) for m in range(rows // FT)]
 
@@ -250,19 +261,13 @@
 
     ahead = z_of(*items[0])
     for step, (j, m) in enumerate(items):
-        z = ahead + biases[j]
+        now = ahead
         if step + 1 < len(items):
             ahead = z_of(*items[step + 1])
-        square = z * z
-        tanh = jnp.tanh(z * (GELU_A + (GELU_A * GELU_B) * square))
-        half = 0.5 * z
-        rise = 0.5 + 0.5 * tanh
-        span = (slice(m * FT, (m + 1) * FT), slice(j * units, (j + 1) * units))
-        act_ref[span] = (z * rise).astype(BF)
-        slope_ref[span] = rise + half * (1.0 - tanh * tanh) * (GELU_A + (3 * GELU_A * GELU_B) * square)
-        if m == rows // FT - 1:
-            copies.send(act_ref.at[:, span[1]], act_any.at[:, span[1]])
-            copies.send(slope_ref.at[:, span[1]], slope_any.at[:, span[1]])
+        for n in range(FT // SLAB):
+            z = now[n * SLAB : (n + 1) * SLAB] + biases[j]
+            rise, _ = rise_of(z)
+            act_ref[m * FT + n * SLAB : m * FT + (n + 1) * SLAB, j * units : (j + 1) * units] = (z * rise).astype(BF)
     wait_all(down)
     hidden.wait()
     for m in range(rows // FT):
@@ -280,11 +285,11 @@
 
 
 def feed_kernel(
-    ids_ref, alpha_ref, acol_ref,
+    ids_ref, alpha_ref, b0_ref, b1_ref, b2_ref, b3_ref, acol_ref,
     arr_any, wu0_any, wu1_any, wu2_any, wu3_any, wd0_any, wd1_any, wd2_any, wd3_any,
-    wo0_any, wo1_any, wo2_any, wo3_any, act_any, slope_any, low_any, f_any, attn_any, o_any,
+    wo0_any, wo1_any, wo2_any, wo3_any, low_any, f_any, attn_any, o_any,
     small_ref, go_any, gh_any, keep_any, send_any,
-    sems, arr_ref, wu_ref, wd_ref, wo_ref, act_ref, slope_ref, low_ref, f_ref, attn_ref, o_ref,
+    sems, arr_ref, wu_ref, wd_ref, wo_ref, act_ref, low_ref, f_ref, attn_ref, o_ref,
     hot_ref, g_ref, gf_ref, gz_ref, gh_ref, ga_ref, go_ref, keep_ref, part_ref, w_ref,
 ):
     me, tensor = ids_ref[0], ids_ref[1]
@@ -295,15 +300,14 @@
     own = me % blocks
     copies = Copies(sems)
     first = copies.start(arr_any, arr_ref)
-    down, slopes, up, later = [], [], [], []
-    for j, wd in enumerate((wd0_any, wd1_any, wd2_any, wd3_any)):
+    lowed = copies.start(low_any, low_ref)
+    down, up, later = [], [], []
+    for j, (wu, wd) in enumerate(
+        ((wu0_any, wd0_any), (wu1_any, wd1_any), (wu2_any, wd2_any), (wu3_any, wd3_any))
+    ):
         span = slice(j * units, (j + 1) * units)
+        up.append(copies.start(wu, wu_ref.at[:, span]))
         down.append(copies.start(wd, wd_ref.at[span, :]))
-        slopes.append(copies.start(slope_any.at[:, span], slope_ref.at[:, span]))
-    for j, wu in enumerate((wu0_any, wu1_any, wu2_any, wu3_any)):
-        up.append(copies.start(wu, wu_ref.at[:, j * units : (j + 1) * units]))
-    lowed = copies.start(low_any, low_ref)
-    acted = copies.start(act_any, act_ref)
     for j, wo in enumerate((wo0_any, wo1_any, wo2_any, wo3_any)):
         place = pl.multiple_of(lax.bitwise_xor(tensor, j) * lanes, LANES)
         later.append(copies.start(wo, wo_ref.at[pl.ds(place, lanes), :]))
@@ -319,21 +323,29 @@
         gf_ref[span, :] = (alpha_ref[1] * grad).astype(BF)
     items = [(j, m) for j in range(len(up)) for m in range(rows // FT)]
 
-    def ga_of(j, m):
+    biases = unit_biases((b0_ref, b1_ref, b2_ref, b3_ref), units)
+    lowed.wait()
+
+    def both_of(j, m):
         if m == 0:
+            up[j].wait()
             down[j].wait()
-        return dot(gf_ref[m * FT : (m + 1) * FT, :], wd_ref[j * units : (j + 1) * units, :], NT)
-
-    ahead = ga_of(*items[0])
+        span, unit = slice(m * FT, (m + 1) * FT), slice(j * units, (j + 1) * units)
+        return dot(low_ref[span, :], wu_ref[:, unit]), dot(gf_ref[span, :], wd_ref[unit, :], NT)
+
+    ahead = both_of(*items[0])
     for step, (j, m) in enumerate(items):
         now = ahead
         if step + 1 < len(items):
-            ahead = ga_of(*items[step + 1])
-        if m == 0:
-            slopes[j].wait()
-        span = (slice(m * FT, (m + 1) * FT), slice(j * units, (j + 1) * units))
-        gz_ref[span] = (now * slope_ref[span]).astype(BF)
-    wait_all(up)
+            ahead = both_of(*items[step + 1])
+        for n in range(FT // SLAB):
+            slab = slice(n * SLAB, (n + 1) * SLAB)
+            z = now[0][slab] + biases[j]
+            rise, square = rise_of(z)
+            slope = rise + z * (rise - rise * rise) * ((2 * GELU_A) + (6 * GELU_A * GELU_B) * square)
+            span = (slice(m * FT + n * SLAB, m * FT + (n + 1) * SLAB), slice(j * units, (j + 1) * units))
+            act_ref[span] = (z * rise).astype(BF)
+            gz_ref[span] = (now[1][slab] * slope).astype(BF)
     wait_all(later)
     gh_sum = attn_sum = jnp.zeros((1, width), F32)
     for m in range(rows // FT):
@@ -357,8 +369,6 @@
         for b in range(blocks):
             out[j // 2, lax.bitwise_xor(own, b), first_row : first_row + count, :] = value[b * count : (b + 1) * count].astype(out.dtype)
 
-    lowed.wait()
-    acted.wait()
     low_t = low_ref[...].T
     gf_t = gf_ref[...].T
     o_t = o_ref[...].T
@@ -680,7 +690,7 @@
     made = pl.pallas_call(
         body,
         out_shape=[*outs, shape((8, LANES), F32)],
-        in_specs=[smem()] * scalars + vmem(n_in - scalars - ins_any) + [whole] * (ins_any - len(aliases or ())) + [held] * len(aliases or ()) + [whole] * len(before),
+        in_specs=[smem()] * scalars + vmem(n_in - scalars - ins_any) + [whole] * (ins_any - len(aliases or ())) + [held] * len(aliases or ()) + [held if id(d) in marks else whole for d in deps],
         out_specs=vmem(n_out - outs_any) + [held] * (outs_any + 1),
         scratch_shapes=list(scratch),
         input_output_aliases=aliases or {},
@@ -781,26 +791,26 @@
     )
     held = lax.optimization_barrier((*far[3:], logs))[:2]
     wu4, wd4 = [four(w, f) for w, f in zip(own[3:], held)]
-    ys, act, slope, branch = call(
+    ys, branch = call(
         forward_kernel,
         (rezero_alphas, *bias4, down_bias.reshape(1, width), arow, low, h, *wu4, *wd4),
-        [shape((rows, width), BF), shape((rows, ff), BF), shape((rows, ff), F32), shape((rows, width), F32)],
-        [sems(40), v16(rows, width), v32(rows, width), v16(width, ff), v16(ff, width), v16(rows, ff), v32(rows, ff),
+        [shape((rows, width), BF), shape((rows, width), F32)],
+        [sems(40), v16(rows, width), v32(rows, width), v16(width, ff), v16(ff, width), v16(rows, ff),
          v32(rows, width), v16(rows, width), hot, v16(rows, width)],
-        scalars=1, ins_any=10, outs_any=4, us=C["forward"], limit=60,
+        scalars=1, ins_any=10, outs_any=2, us=C["forward"], limit=60,
     )
     bundle = (width + units + lanes) // blocks
     part = shape((tensors // 2, blocks, bundle, width), BF)
     small1, go, gh, keep1, send1 = call(
         feed_kernel,
-        (ids, rezero_alphas, acol, arr_g, *wu4, *wd4, *wo4, act, slope, low, branch, attn, o),
+        (ids, rezero_alphas, *bias4, acol, arr_g, *wu4, *wd4, *wo4, low, branch, attn, o),
         [shape((8, width), F32), shape((rows, width), BF), shape((rows, width), F32),
          shape(part.shape, F32), part],
-        [sems(48), v16(rows, width), v16(width, ff), v16(ff, width), v16(width, width), v16(rows, ff), v32(rows, ff),
+        [sems(48), v16(rows, width), v16(width, ff), v16(ff, width), v16(width, width), v16(rows, ff),
          v16(rows, width), v32(rows, width), v32(rows, width), v16(rows, width),
          hot, v16(rows, width), v16(rows, width), v16(rows, ff), v32(rows, width), v16(rows, width), v16(rows, width),
          v32(*part.shape), v16(*part.shape), v32(width, width)],
-        scalars=2, ins_any=19, outs_any=4, us=C["feed"], deps=(ys,), limit=60,
+        scalars=2, ins_any=17, outs_any=4, us=C["feed"], deps=(ys,), limit=60,
     )
     arr_y = exchange(ys)
     got = across("tensor", 1, send1)
@@ -855,12 +865,6 @@
     y_own = settle(arr_y, (grad_b,))
     y_far = across("tensor", 2, y_own)
     y_core = across("tensor", 1, y_own)
-    n = n // 2
-    keep1, send1 = call(
-        functools.partial(halve_kernel, low_half), (keep1, got_y), [blocks_of(n, keep1, F32), blocks_of(n, keep1, BF)],
-        deps=(y_own,), us=C["halve"],
-    )
-    got_x = across("tensor", 2, send1)
     share = (3 * width) // blocks
     split = 2 * 16 * width // LANES
     n2 = half * blocks
@@ -869,12 +873,18 @@
         [bare, shape((n2, share, lanes), F32), shape((n2 + 1, share, lanes), BF)],
         [sems(20), v16(rows, 3 * width), v16(rows, width), v32(n2, share, lanes), v16(n2, share, lanes), v32(width, 3 * width),
          v16(split, LANES)],
-        scalars=1, ins_any=3, outs_any=2, us=C["weight"], deps=(keep1,), limit=60,
-    )
+        scalars=1, ins_any=3, outs_any=2, us=C["weight"], deps=(y_own,), limit=60,
+    )
+    n = n // 2
+    keep1, send1 = call(
+        functools.partial(halve_kernel, low_half), (keep1, got_y), [blocks_of(n, keep1, F32), blocks_of(n, keep1, BF)],
+        deps=(small,), us=C["halve"],
+    )
+    got_x = across("tensor", 2, send1)
     gxs = call(
         last_kernel, (ids, arow, grad_a, grad_b, gh, *wa4), [shape((rows, width), BF)],
         [sems(40), v16(rows, 3 * width), v32(rows, width), v16(width, 3 * width), hot, v16(rows, width), v16(rows, width)],
-        scalars=1, ins_any=7, outs_any=1, us=C["last"], deps=(small,), limit=60,
+        scalars=1, ins_any=7, outs_any=1, us=C["last"], deps=(keep1,), limit=60,
     )[0]
     arr_gx = exchange(gxs)
     got = across("tensor", 1, send2)

time: 282 us -> 275 us (0.975)
  waiting for transfers between devices: 76.2 us -> 69.9 us
    ppermute x36, waiting for transfers between devices: 52.3 us -> 43.4 us  [across(): return lax.ppermute(value, axis, [(i, i ^ bit) for i in range(count)])]
    all_to_all x4, waiting for transfers between devices: 15.1 us -> 18.7 us  [exchange(): lax.all_to_all(rows_out.reshape(groups, rows // groups, width), 'dp', 0,...]
    unnamed x76 -> x84, local copies, waits for them, and re-layouts: 14.3 us -> 16.3 us
  transfers between devices with their start and end apart: 41 -> 41, of which waited for: 17 -> 15; matrix products, arithmetic and copies ran while one was open for 1% -> 1% of each run, Pallas kernels for 36% -> 35%
where the time goes in v1:
time: 275 us; the launch traced here: 270 us
  Pallas kernels  126 us (46%)
  waiting for transfers between devices  69.9 us (25%)
  starting transfers between devices  52.5 us (19%)
  local copies, waits for them, and re-layouts  18.9 us (7%)
    pallas_call x25, Pallas kernels, call(): pl.pallas_call(body, out_shape=[*outs, shape((8, LANES), F32)], in_specs=...  115 us
    ppermute x36, waiting for transfers between devices, across(): return lax.ppermute(value, axis, [(i, i ^ bit) for i in range(count)])  43.4 us
    ppermute x36, starting transfers between devices, across(): return lax.ppermute(value, axis, [(i, i ^ bit) for i in range(count)])  26.9 us
    all_to_all x4, starting transfers between devices, exchange(): lax.all_to_all(rows_out.reshape(groups, rows // groups, width), 'dp', 0,...  22.1 us
    all_to_all x4, waiting for transfers between devices, exchange(): lax.all_to_all(rows_out.reshape(groups, rows // groups, width), 'dp', 0,...  18.7 us
    unnamed x84, local copies, waits for them, and re-layouts  16.3 us
    all_to_all x1, waiting for transfers between devices, per_device(): lax.all_to_all(shared, 'dp', 0, 0, tiled=True, axis_index_groups=ranks)  7.77 us
    pallas_call x1, Pallas kernels, per_device(): by_micro(functools.partial(route_kernel, groups), 0, [shape((rows, width)...  6.25 us
  transfers between devices with their start and end apart: 41, of which 15 were waited for; matrix products, arithmetic and copies ran while one was open for 1% of the time, Pallas kernels for 35%

profile of v1, /device:TPU:0, one launch (start us, length us, event | category | flops | bytes accessed | tf_op | source)
XLA Modules:
  0.0 269.6 jit_solution(12670234706501907906)
XLA Ops:
  1.2 6.2 %shard_map.212 = (bf16[1024,512]{1,0:T(8,128)(2,1)}, s32[8,128]{1,0:T(8,128)}, s32[1024,128]{1,0:T(8,128)}) custom-call(s32[2]{0:T(128)} %pad_add_fusion.ids_ref.refs_0_, s32[4,8192]{1,0:T(4,128)} %src_ref.3, bf16[4,1024,512]{2,1,0:T(8,128)(2,1)} %x_ref.1), custom_call_target="tpu_custom_call" | custom-call | flops 6000000000 | tf_op jit(solution)/shard_map/pallas_call | solution.py:747
  7.5 7.3 %all-to-all-start = ((bf16[8,128,512]{2,1,0:T(8,128)(2,1)}), bf16[8,128,512]{2,1,0:T(8,128)(2,1)S(1)}, u32[]{:S(2)}, u32[]{:S(2)}) async-start(bf16[8,128,512]{2,1,0:T(8,128)(2,1)} %bitcast.21), calls=%async_computation | async-start | bytes 2097152 | tf_op jit(solution)/shard_map/all_to_all | solution.py:753
  18.5 4.9 %shard_map.213 = (bf16[1024,512]{1,0:T(8,128)(2,1)}, s32[8,1024]{1,0:T(8,128)}, s32[1024,128]{1,0:T(8,128)}) custom-call(s32[2]{0:T(128)} %pad_add_fusion.ids_ref.refs_0_, s32[4,8192]{1,0:T(4,128)} %src_ref.3, bf16[4,1024,512]{2,1,0:T(8,128)(2,1)} %g_ref.1, s32[8,128]{1,0:T(8,128)} %get-tuple-element.95.srow_ref), custom_call_target="tpu_custom_call" | custom-call | flops 6000000000 | tf_op jit(solution)/shard_map/pallas_call | solution.py:756
  23.4 3.5 %collective-permute-done.1.refs_5_.refs_3_.refs_4_ = bf16[8,128]{1,0:T(8,128)(2,1)S(1)} collective-permute-done((bf16[8,128]{1,0:T(8,128)(2,1)S(1)}, bf16[8,128]{1,0:T(8,128)(2,1)S(1)}, u32[]{:S(2)}, u32[]{:S(2)}) %collective-permute-start.1) | collective-permute-done | bytes 2080 | tf_op jit(solution)/shard_map/ppermute | solution.py:722
  34.3 6.2 %all-to-all-done = bf16[8,128,512]{2,1,0:T(8,128)(2,1)S(1)} async-done(((bf16[8,128,512]{2,1,0:T(8,128)(2,1)}), bf16[8,128,512]{2,1,0:T(8,128)(2,1)S(1)}, u32[]{:S(2)}, u32[]{:S(2)}) %all-to-all-start) | async-done | bytes 1048608 | tf_op jit(solution)/shard_map/all_to_all | solution.py:753
  40.6 3.9 %all-to-all-start.2 = ((bf16[8,128,512]{2,1,0:T(8,128)(2,1)}), bf16[8,128,512]{2,1,0:T(8,128)(2,1)S(1)}, u32[]{:S(2)}, u32[]{:S(2)}) async-start(bf16[8,128,512]{2,1,0:T(8,128)(2,1)} %bitcast.19), calls=%async_computation.2 | async-start | bytes 2097152 | tf_op jit(solution)/shard_map/all_to_all | solution.py:753
  44.5 18.6 %shard_map.214 = (f32[8,1024]{1,0:T(8,128)}, bf16[1024,512]{1,0:T(8,128)(2,1)}, bf16[1024,512]{1,0:T(8,128)(2,1)}, bf16[1024,512]{1,0:T(8,128)(2,1)}, bf16[1024,...) custom-call(s32[2]{0:T(128)} %pad_add_fusion.ids_ref.refs_0_, ...), custom_call_target="tpu_custom_call" | custom-call | flops 19000000512 | tf_op jit(solution)/shard_map/pallas_call | solution.py:690
  66.9 10.5 %shard_map.215 = (bf16[1024,512]{1,0:T(8,128)(2,1)}, f32[1024,512]{1,0:T(8,128)}, f32[8,128]{1,0:T(8,128)}) custom-call(f32[2]{0:T(128)} %refs_1_.1, bf16[8,128]{1,0:T(8,128)(2,1)} %copy-done.24, bf16[8,128]{1,0:T(8,128)(2,1)} %copy-done.40, bf16[8,128]{1,0:T(8,128)(2,1)} %copy-done.39, bf16[8,128]{1,0:T(8,128)(2,1)} %copy-done.41, ...), custom_call_target="tpu_custom_call" | custom-call | flops 5000000000 | tf_op jit(solution)/shard_map/pallas_call | solution.py:690
  78.4 21.7 %shard_map.216 = (f32[8,512]{1,0:T(8,128)}, bf16[1024,512]{1,0:T(8,128)(2,1)}, f32[1024,512]{1,0:T(8,128)}, f32[2,8,144,512]{3,2,1,0:T(8,128)}, bf16[2,8,144,512]{3,2,1,0:T(8,128)(2,1)}, /*index=5*/f32[8,128]{1,0:T(8,128)}) custom-call(s32[2]{0:T(128)} %pad_add_fusion.ids_ref.refs_0_, f32[2]{0:T(128)} %refs_1_.1, bf16[8,128]{1,0:T(8,128)(2,1)} %copy-done.24, ...), custom_call_target="tpu_custom_call" | custom-call | flops 19000000512 | tf_op jit(solution)/shard_map/pallas_call | solution.py:690
  100.3 6.2 %all-to-all-start.1 = ((bf16[8,128,512]{2,1,0:T(8,128)(2,1)}), bf16[8,128,512]{2,1,0:T(8,128)(2,1)S(1)}, u32[]{:S(2)}, u32[]{:S(2)}) async-start(bf16[8,128,512]{2,1,0:T(8,128)(2,1)} %bitcast.24), calls=%async_computation.1 | async-start | bytes 2097152 | tf_op jit(solution)/shard_map/all_to_all | solution.py:753
  106.5 2.3 copy-done.2
  114.2 11.0 %shard_map.218 = (bf16[3,1024,256]{2,1,0:T(8,128)(2,1)}, f32[8,128]{1,0:T(8,128)}) custom-call(s32[3]{0:T(128)} %dynamic-slice_reduce_fusion.refs_1_.refs_0_, f32[8,1024]{1,0:T(8,128)} %get-tuple-element.104.refs_1_, bf16[1024,512]{1,0:T(8,128)(2,1)} %get-tuple-element.109.refs_2_, bf16[1024,512]{1,0:T(8,128)(2,1)} %get-tuple-element.110.refs_3_, ...), custom_call_target="tpu_custom_call" | custom-call | flops 11000000512 | tf_op jit(solution)/shard_map/pallas_call | solution.py:690
  125.2 11.6 %shard_map.219 = (bf16[3,1024,256]{2,1,0:T(8,128)(2,1)}, f32[8,128]{1,0:T(8,128)}) custom-call(s32[3]{0:T(128)} %dynamic-slice_reduce_fusion.refs_1_.refs_0_, f32[8,1024]{1,0:T(8,128)} %get-tuple-element.104.refs_1_, bf16[1024,512]{1,0:T(8,128)(2,1)} %get-tuple-element.109.refs_2_, bf16[1024,512]{1,0:T(8,128)(2,1)} %get-tuple-element.110.refs_3_, ...), custom_call_target="tpu_custom_call" | custom-call | flops 11000000512 | tf_op jit(solution)/shard_map/pallas_call | solution.py:690
  141.9 6.7 %shard_map.221 = (f32[16,512]{1,0:T(8,128)}, f32[16,192,128]{2,1,0:T(8,128)}, bf16[17,192,128]{2,1,0:T(8,128)(2,1)}, f32[8,128]{1,0:T(8,128)}) custom-call(s32[2]{0:T(128)} %pad_add_fusion.ids_ref.refs_0_, f32[8,512]{1,0:T(8,128)} %get-tuple-element.126.refs_1_, bf16[3,1024,256]{2,1,0:T(8,128)(2,1)} %get-tuple-element.127.refs_2_, ...), custom_call_target="tpu_custom_call" | custom-call | flops 200000000 | tf_op jit(solution)/shard_map/pallas_call | solution.py:690
  155.9 7.8 %shard_map.223 = (bf16[1024,512]{1,0:T(8,128)(2,1)}, f32[8,128]{1,0:T(8,128)}) custom-call(s32[2]{0:T(128)} %pad_add_fusion.ids_ref.refs_0_, s32[8,1024]{1,0:T(8,128)} %get-tuple-element.96.refs_6_.refs_1_, bf16[3,1024,256]{2,1,0:T(8,128)(2,1)} %get-tuple-element.127.refs_2_, bf16[3,1024,256]{2,1,0:T(8,128)(2,1)} %get-tuple-element.128.refs_3_, ...), custom_call_target="tpu_custom_call" | custom-call | flops 20000000000 | tf_op jit(solution)/shard_map/pallas_call | solution.py:690
  163.7 4.8 %all-to-all-start.3 = ((bf16[8,128,512]{2,1,0:T(8,128)(2,1)}), bf16[8,128,512]{2,1,0:T(8,128)(2,1)S(1)}, u32[]{:S(2)}, u32[]{:S(2)}) async-start(bf16[8,128,512]{2,1,0:T(8,128)(2,1)} %bitcast.22), calls=%async_computation.3 | async-start | bytes 2097152 | tf_op jit(solution)/shard_map/all_to_all | solution.py:753
  173.1 6.2 %collective-permute-done.18.refs_1_ = bf16[4,144,512]{2,1,0:T(8,128)(2,1)S(1)} collective-permute-done((bf16[4,144,512]{2,1,0:T(8,128)(2,1)}, bf16[4,144,512]{2,1,0:T(8,128)(2,1)S(1)}, u32[]{:S(2)}, u32[]{:S(2)}) %collective-permute-start.18) | collective-permute-done | bytes 589856 | tf_op jit(solution)/shard_map/ppermute | solution.py:722
  181.6 2.4 collective-permute-start.23
  184.6 3.9 %shard_map.227 = (f32[4,1024,512]{2,1,0:T(8,128)}, f32[8,128]{1,0:T(8,128)S(1)}) custom-call(s32[2]{0:T(128)S(1)} %copy-done.4, bf16[1024,512]{1,0:T(8,128)(2,1)} %get-tuple-element.123.refs_1_, bf16[1024,512]{1,0:T(8,128)(2,1)} %collective-permute-done.21.refs_2_, f32[8,128]{1,0:T(8,128)S(1)} %get-tuple-element.141.refs_1_.refs_3_), custom_call_target="tpu_custom_call" | custom-call | flops 5000000000 | tf_op jit(solution)/shard_map/pallas_call | solution.py:690
  189.4 12.5 %all-to-all-done.3 = bf16[8,128,512]{2,1,0:T(8,128)(2,1)S(1)} async-done(((bf16[8,128,512]{2,1,0:T(8,128)(2,1)}), bf16[8,128,512]{2,1,0:T(8,128)(2,1)S(1)}, u32[]{:S(2)}, u32[]{:S(2)}) %all-to-all-start.3) | async-done | bytes 1048608 | tf_op jit(solution)/shard_map/all_to_all | solution.py:753
  203.0 2.3 shard_map.229
  205.3 3.5 %all-to-all-start.4 = ((bf16[8,320,128]{2,1,0:T(8,128)(2,1)}), bf16[8,320,128]{2,1,0:T(8,128)(2,1)S(1)}, u32[]{:S(2)}, u32[]{:S(2)}) async-start(bf16[8,320,128]{2,1,0:T(8,128)(2,1)} %get-tuple-element.160), calls=%async_computation.4 | async-start | bytes 1310720 | tf_op jit(solution)/shard_map/all_to_all | solution.py:908
  211.4 3.9 %shard_map.231 = (f32[4,1024,512]{2,1,0:T(8,128)}, f32[8,128]{1,0:T(8,128)S(1)}) custom-call(s32[2]{0:T(128)S(1)} %copy-done.4, bf16[1024,512]{1,0:T(8,128)(2,1)S(1)} %get-tuple-element.142.refs_1_, bf16[1024,512]{1,0:T(8,128)(2,1)} %collective-permute-done.20.refs_2_, f32[4,1024,512]{2,1,0:T(8,128)} %get-tuple-element.143.refs_3_, ...), custom_call_target="tpu_custom_call", output_to_operand_aliasing={{0}: (3, {})} | custom-call | flops 5000000000 | tf_op jit(solution)/shard_map/pallas_call | solution.py:690
  215.3 3.9 %shard_map.232 = (f32[4,1024,512]{2,1,0:T(8,128)}, f32[8,128]{1,0:T(8,128)S(1)}) custom-call(s32[2]{0:T(128)S(1)} %copy-done.4, bf16[1024,512]{1,0:T(8,128)(2,1)} %get-tuple-element.158.refs_1_, bf16[1024,512]{1,0:T(8,128)(2,1)} %collective-permute-done.27.refs_2_, f32[8,128]{1,0:T(8,128)S(1)} %get-tuple-element.161.refs_3_), custom_call_target="tpu_custom_call" | custom-call | flops 5000000000 | tf_op jit(solution)/shard_map/pallas_call | solution.py:690
  219.3 7.8 %all-to-all-done.4.refs_1_ = bf16[8,320,128]{2,1,0:T(8,128)(2,1)S(1)} async-done(((bf16[8,320,128]{2,1,0:T(8,128)(2,1)}), bf16[8,320,128]{2,1,0:T(8,128)(2,1)S(1)}, u32[]{:S(2)}, u32[]{:S(2)}) %all-to-all-start.4) | async-done | bytes 655392 | tf_op jit(solution)/shard_map/all_to_all | solution.py:908
  230.7 7.7 %collective-permute-done.28.refs_0_ = bf16[192,512]{1,0:T(8,128)(2,1)S(1)} collective-permute-done((bf16[192,512]{1,0:T(8,128)(2,1)S(1)}, bf16[192,512]{1,0:T(8,128)(2,1)S(1)}, u32[]{:S(2)}, u32[]{:S(2)}) %collective-permute-start.28) | collective-permute-done | bytes 196640 | tf_op jit(solution)/shard_map/ppermute | solution.py:722
  239.4 5.8 %collective-permute-done.31.refs_1_.refs_2_.refs_8_ = bf16[192,512]{1,0:T(8,128)(2,1)S(1)} collective-permute-done((bf16[192,512]{1,0:T(8,128)(2,1)S(1)}, bf16[192,512]{1,0:T(8,128)(2,1)S(1)}, u32[]{:S(2)}, u32[]{:S(2)}) %collective-permute-start.31) | collective-permute-done | bytes 196640 | tf_op jit(solution)/shard_map/ppermute | solution.py:722
  246.4 6.1 %collective-permute-done.33.refs_1_.refs_7_ = bf16[192,512]{1,0:T(8,128)(2,1)S(1)} collective-permute-done((bf16[192,512]{1,0:T(8,128)(2,1)S(1)}, bf16[192,512]{1,0:T(8,128)(2,1)S(1)}, u32[]{:S(2)}, u32[]{:S(2)}) %collective-permute-start.33) | collective-permute-done | bytes 196640 | tf_op jit(solution)/shard_map/ppermute | solution.py:722
  254.6 5.8 %collective-permute-done.34.refs_5_ = bf16[192,512]{1,0:T(8,128)(2,1)S(1)} collective-permute-done((bf16[192,512]{1,0:T(8,128)(2,1)S(1)}, bf16[192,512]{1,0:T(8,128)(2,1)S(1)}, u32[]{:S(2)}, u32[]{:S(2)}) %collective-permute-start.34) | collective-permute-done | bytes 196640 | tf_op jit(solution)/shard_map/ppermute | solution.py:722
  260.3 2.9 %collective-permute-done.35.refs_9_ = bf16[192,512]{1,0:T(8,128)(2,1)S(1)} collective-permute-done((bf16[192,512]{1,0:T(8,128)(2,1)S(1)}, bf16[192,512]{1,0:T(8,128)(2,1)S(1)}, u32[]{:S(2)}, u32[]{:S(2)}) %collective-permute-start.35) | collective-permute-done | bytes 196640 | tf_op jit(solution)/shard_map/ppermute | solution.py:722
  263.3 2.6 shard_map.238
  266.5 2.8 %shard_map.236 = (f32[4,1024,512]{2,1,0:T(8,128)}, f32[8,128]{1,0:T(8,128)}) custom-call(s32[2]{0:T(128)S(1)} %copy-done.4, bf16[1024,512]{1,0:T(8,128)(2,1)S(1)} %get-tuple-element.165.refs_1_, bf16[1024,512]{1,0:T(8,128)(2,1)S(1)} %collective-permute-done.32.refs_2_, f32[4,1024,512]{2,1,0:T(8,128)} %get-tuple-element.166.refs_3_), custom_call_target="tpu_custom_call", output_to_operand_aliasing={{0}: (3, {})} | custom-call | flops 5000000000 | tf_op jit(solution)/shard_map/pallas_call | solution.py:690
  (169 shorter events, 54.9 us)
Async XLA Ops:
  7.5 33.0 %all-to-all-start = ((bf16[8,128,512]{2,1,0:T(8,128)(2,1)}), bf16[8,128,512]{2,1,0:T(8,128)(2,1)S(1)}, u32[]{:S(2)}, u32[]{:S(2)}) async-start(bf16[8,128,512]{2,1,0:T(8,128)(2,1)} %bitcast.21), calls=%async_computation | async-start | bytes 2097152 | tf_op jit(solution)/shard_map/all_to_all | solution.py:753
  14.8 13.5 %collective-permute-start.2 = (bf16[3,512,128]{2,1,0:T(8,128)(2,1)S(1)}, bf16[3,512,128]{2,1,0:T(8,128)(2,1)}, u32[]{:S(2)}, u32[]{:S(2)}) collective-permute-start(bf16[3,512,128]{2,1,0:T(8,128)(2,1)S(1)} %copy-done.33), channel_id=1, source_target_pairs={{0,2},{1,3},{2,0},{3,1},{4,6},{5,7},{6,4},{7,5},{8,10},{9,11},{10,... | collective-permute-start | bytes 1179656 | tf_op jit(solution)/shard_map/ppermute | solution.py:722
  16.3 15.9 %collective-permute-start.5 = (bf16[3,512,128]{2,1,0:T(8,128)(2,1)S(1)}, bf16[3,512,128]{2,1,0:T(8,128)(2,1)S(1)}, u32[]{:S(2)}, u32[]{:S(2)}) collective-permute-start(bf16[3,512,128]{2,1,0:T(8,128)(2,1)S(1)} %copy-done.33), channel_id=1, source_target_pairs={{0,1},{1,0},{2,3},{3,2},{4,5},{5,4},{6,7},{7,6},{8,9},{9,8},{10,11... | collective-permute-start | bytes 1179656 | tf_op jit(solution)/shard_map/ppermute | solution.py:722
  16.5 10.4 %collective-permute-start.1 = (bf16[8,128]{1,0:T(8,128)(2,1)S(1)}, bf16[8,128]{1,0:T(8,128)(2,1)S(1)}, u32[]{:S(2)}, u32[]{:S(2)}) collective-permute-start(bf16[8,128]{1,0:T(8,128)(2,1)S(1)} %maximum_maximum_fusion.refs_3_.refs_1_.refs_2_), channel_id=1, source_target_pairs={{0,2},{1,3},{2,0},{3,1},{4,6},{5,7},{6,4},{7,5},{8,10},{9,11},{10,... | collective-permute-start | bytes 6152 | tf_op jit(solution)/shard_map/ppermute | solution.py:722
  17.0 11.2 %collective-permute-start.3 = (bf16[128,512]{1,0:T(8,128)(2,1)S(1)}, bf16[128,512]{1,0:T(8,128)(2,1)S(1)}, u32[]{:S(2)}, u32[]{:S(2)}) collective-permute-start(bf16[128,512]{1,0:T(8,128)(2,1)S(1)} %copy-done.35), channel_id=1, source_target_pairs={{0,2},{1,3},{2,0},{3,1},{4,6},{5,7},{6,4},{7,5},{8,10},{9,11},{10,... | collective-permute-start | bytes 393224 | tf_op jit(solution)/shard_map/ppermute | solution.py:722
  28.3 16.2 %collective-permute-start.6 = (bf16[3,512,128]{2,1,0:T(8,128)(2,1)}, bf16[3,512,128]{2,1,0:T(8,128)(2,1)}, u32[]{:S(2)}, u32[]{:S(2)}) collective-permute-start(bf16[3,512,128]{2,1,0:T(8,128)(2,1)} %collective-permute-done.2.refs_12_.refs_7_), channel_id=1, source_target_pairs={{0,1},{1,0},{2,3},{3,2},{4,5},{5,4},{6,7},{7,6},{8,9},{9,8},{10,11... | collective-permute-start | bytes 1179656 | tf_op jit(solution)/shard_map/ppermute | solution.py:722
  31.9 32.4 %collective-permute-start.9 = (bf16[512,512]{1,0:T(8,128)(2,1)S(1)}, bf16[512,512]{1,0:T(8,128)(2,1)}, u32[]{:S(2)}, u32[]{:S(2)}) collective-permute-start(bf16[512,512]{1,0:T(8,128)(2,1)S(1)} %copy-done.29), channel_id=1, source_target_pairs={{0,1},{1,0},{2,3},{3,2},{4,5},{5,4},{6,7},{7,6},{8,9},{9,8},{10,11... | collective-permute-start | bytes 1572872 | tf_op jit(solution)/shard_map/ppermute | solution.py:722
  32.2 30.9 %collective-permute-start.10 = (bf16[512,512]{1,0:T(8,128)(2,1)S(1)}, bf16[512,512]{1,0:T(8,128)(2,1)}, u32[]{:S(2)}, u32[]{:S(2)}) collective-permute-start(bf16[512,512]{1,0:T(8,128)(2,1)S(1)} %copy-done.29), channel_id=1, source_target_pairs={{0,2},{1,3},{2,0},{3,1},{4,6},{5,7},{6,4},{7,5},{8,10},{9,11},{10,... | collective-permute-start | bytes 1572872 | tf_op jit(solution)/shard_map/ppermute | solution.py:722
  33.7 29.4 %collective-permute-start.11 = (bf16[512,512]{1,0:T(8,128)(2,1)S(1)}, bf16[512,512]{1,0:T(8,128)(2,1)}, u32[]{:S(2)}, u32[]{:S(2)}) collective-permute-start(bf16[512,512]{1,0:T(8,128)(2,1)S(1)} %copy-done.30), channel_id=1, source_target_pairs={{0,2},{1,3},{2,0},{3,1},{4,6},{5,7},{6,4},{7,5},{8,10},{9,11},{10,... | collective-permute-start | bytes 1572872 | tf_op jit(solution)/shard_map/ppermute | solution.py:722
  34.3 30.0 %collective-permute-start.13 = (bf16[512,512]{1,0:T(8,128)(2,1)S(1)}, bf16[512,512]{1,0:T(8,128)(2,1)}, u32[]{:S(2)}, u32[]{:S(2)}) collective-permute-start(bf16[512,512]{1,0:T(8,128)(2,1)S(1)} %copy-done.30), channel_id=1, source_target_pairs={{0,1},{1,0},{2,3},{3,2},{4,5},{5,4},{6,7},{7,6},{8,9},{9,8},{10,11... | collective-permute-start | bytes 1572872 | tf_op jit(solution)/shard_map/ppermute | solution.py:722
  40.6 36.8 %all-to-all-start.2 = ((bf16[8,128,512]{2,1,0:T(8,128)(2,1)}), bf16[8,128,512]{2,1,0:T(8,128)(2,1)S(1)}, u32[]{:S(2)}, u32[]{:S(2)}) async-start(bf16[8,128,512]{2,1,0:T(8,128)(2,1)} %bitcast.19), calls=%async_computation.2 | async-start | bytes 2097152 | tf_op jit(solution)/shard_map/all_to_all | solution.py:753
  100.3 36.6 %all-to-all-start.1 = ((bf16[8,128,512]{2,1,0:T(8,128)(2,1)}), bf16[8,128,512]{2,1,0:T(8,128)(2,1)S(1)}, u32[]{:S(2)}, u32[]{:S(2)}) async-start(bf16[8,128,512]{2,1,0:T(8,128)(2,1)} %bitcast.24), calls=%async_computation.1 | async-start | bytes 2097152 | tf_op jit(solution)/shard_map/all_to_all | solution.py:753
  112.2 37.0 %collective-permute-start.17 = (bf16[8,144,512]{2,1,0:T(8,128)(2,1)}, bf16[8,144,512]{2,1,0:T(8,128)(2,1)}, u32[]{:S(2)}, u32[]{:S(2)}) collective-permute-start(bf16[8,144,512]{2,1,0:T(8,128)(2,1)} %get-tuple-element.125), channel_id=1, source_target_pairs={{0,4},{4,0},{8,12},{12,8},{16,20},{20,16},{24,28},{28,24},{1,5},{5... | collective-permute-start | bytes 3538952 | tf_op jit(solution)/shard_map/ppermute | solution.py:722
  140.4 32.7 %collective-permute-start.16 = (bf16[1024,512]{1,0:T(8,128)(2,1)}, bf16[1024,512]{1,0:T(8,128)(2,1)S(1)}, u32[]{:S(2)}, u32[]{:S(2)}) collective-permute-start(bf16[1024,512]{1,0:T(8,128)(2,1)} %get-tuple-element.123.refs_1_), channel_id=1, source_target_pairs={{0,2},{1,3},{2,0},{3,1},{4,6},{5,7},{6,4},{7,5},{8,10},{9,11},{10,... | collective-permute-start | bytes 3145736 | tf_op jit(solution)/shard_map/ppermute | solution.py:722
  141.9 42.1 %collective-permute-start.21 = (bf16[1024,512]{1,0:T(8,128)(2,1)}, bf16[1024,512]{1,0:T(8,128)(2,1)}, u32[]{:S(2)}, u32[]{:S(2)}) collective-permute-start(bf16[1024,512]{1,0:T(8,128)(2,1)} %get-tuple-element.123.refs_1_), channel_id=1, source_target_pairs={{0,1},{1,0},{2,3},{3,2},{4,5},{5,4},{6,7},{7,6},{8,9},{9,8},{10,11... | collective-permute-start | bytes 3145736 | tf_op jit(solution)/shard_map/ppermute | solution.py:722
  148.6 19.9 %collective-permute-start.19 = (bf16[17,192,128]{2,1,0:T(8,128)(2,1)}, bf16[17,192,128]{2,1,0:T(8,128)(2,1)S(1)}, u32[]{:S(2)}, u32[]{:S(2)}) collective-permute-start(bf16[17,192,128]{2,1,0:T(8,128)(2,1)} %get-tuple-element.136), channel_id=1, source_target_pairs={{0,1},{1,0},{2,3},{3,2},{4,5},{5,4},{6,7},{7,6},{8,9},{9,8},{10,11... | collective-permute-start | bytes 2506760 | tf_op jit(solution)/shard_map/ppermute | solution.py:722
  155.4 23.9 %collective-permute-start.18 = (bf16[4,144,512]{2,1,0:T(8,128)(2,1)}, bf16[4,144,512]{2,1,0:T(8,128)(2,1)S(1)}, u32[]{:S(2)}, u32[]{:S(2)}) collective-permute-start(bf16[4,144,512]{2,1,0:T(8,128)(2,1)} %get-tuple-element.133), channel_id=1, source_target_pairs={{0,2},{1,3},{2,0},{3,1},{4,6},{5,7},{6,4},{7,5},{8,10},{9,11},{10,... | collective-permute-start | bytes 1769480 | tf_op jit(solution)/shard_map/ppermute | solution.py:722
  163.7 38.2 %all-to-all-start.3 = ((bf16[8,128,512]{2,1,0:T(8,128)(2,1)}), bf16[8,128,512]{2,1,0:T(8,128)(2,1)S(1)}, u32[]{:S(2)}, u32[]{:S(2)}) async-start(bf16[8,128,512]{2,1,0:T(8,128)(2,1)} %bitcast.22), calls=%async_computation.3 | async-start | bytes 2097152 | tf_op jit(solution)/shard_map/all_to_all | solution.py:753
  171.5 17.0 %collective-permute-start.25 = (bf16[9,192,128]{2,1,0:T(8,128)(2,1)S(1)}, bf16[9,192,128]{2,1,0:T(8,128)(2,1)S(1)}, u32[]{:S(2)}, u32[]{:S(2)}) collective-permute-start(bf16[9,192,128]{2,1,0:T(8,128)(2,1)S(1)} %get-tuple-element.151), channel_id=1, source_target_pairs={{0,2},{1,3},{2,0},{3,1},{4,6},{5,7},{6,4},{7,5},{8,10},{9,11},{10,... | collective-permute-start | bytes 1327112 | tf_op jit(solution)/shard_map/ppermute | solution.py:722
  180.1 31.3 %collective-permute-start.20 = (bf16[1024,512]{1,0:T(8,128)(2,1)S(1)}, bf16[1024,512]{1,0:T(8,128)(2,1)}, u32[]{:S(2)}, u32[]{:S(2)}) collective-permute-start(bf16[1024,512]{1,0:T(8,128)(2,1)S(1)} %get-tuple-element.142.refs_1_), channel_id=1, source_target_pairs={{0,1},{1,0},{2,3},{3,2},{4,5},{5,4},{6,7},{7,6},{8,9},{9,8},{10,11... | collective-permute-start | bytes 3145736 | tf_op jit(solution)/shard_map/ppermute | solution.py:722
  180.1 28.7 %collective-permute-start.22 = (bf16[144,512]{1,0:T(8,128)(2,1)}, bf16[144,512]{1,0:T(8,128)(2,1)S(1)}, u32[]{:S(2)}, u32[]{:S(2)}) collective-permute-start(bf16[144,512]{1,0:T(8,128)(2,1)} %get-tuple-element.145), channel_id=1, source_target_pairs={{0,8},{4,12},{8,0},{12,4},{16,24},{20,28},{24,16},{28,20},{1,9},{5... | collective-permute-start | bytes 442376 | tf_op jit(solution)/shard_map/ppermute | solution.py:722
  181.6 28.7 %collective-permute-start.23 = (bf16[144,512]{1,0:T(8,128)(2,1)}, bf16[144,512]{1,0:T(8,128)(2,1)S(1)}, u32[]{:S(2)}, u32[]{:S(2)}) collective-permute-start(bf16[144,512]{1,0:T(8,128)(2,1)} %get-tuple-element.146), channel_id=1, source_target_pairs={{0,16},{4,20},{8,24},{12,28},{16,0},{20,4},{24,8},{28,12},{1,17},{... | collective-permute-start | bytes 442376 | tf_op jit(solution)/shard_map/ppermute | solution.py:722
  184.0 26.4 %collective-permute-start.24 = (bf16[144,512]{1,0:T(8,128)(2,1)S(1)}, bf16[144,512]{1,0:T(8,128)(2,1)S(1)}, u32[]{:S(2)}, u32[]{:S(2)}) collective-permute-start(bf16[144,512]{1,0:T(8,128)(2,1)S(1)} %get-tuple-element.147), channel_id=1, source_target_pairs={{0,24},{4,28},{8,16},{12,20},{16,8},{20,12},{24,0},{28,4},{1,25},{... | collective-permute-start | bytes 442376 | tf_op jit(solution)/shard_map/ppermute | solution.py:722
  205.3 10.1 %collective-permute-start.27 = (bf16[1024,512]{1,0:T(8,128)(2,1)}, bf16[1024,512]{1,0:T(8,128)(2,1)}, u32[]{:S(2)}, u32[]{:S(2)}) collective-permute-start(bf16[1024,512]{1,0:T(8,128)(2,1)} %get-tuple-element.158.refs_1_), channel_id=1, source_target_pairs={{0,1},{1,0},{2,3},{3,2},{4,5},{5,4},{6,7},{7,6},{8,9},{9,8},{10,11... | collective-permute-start | bytes 3145736 | tf_op jit(solution)/shard_map/ppermute | solution.py:722
  205.3 21.8 %all-to-all-start.4 = ((bf16[8,320,128]{2,1,0:T(8,128)(2,1)}), bf16[8,320,128]{2,1,0:T(8,128)(2,1)S(1)}, u32[]{:S(2)}, u32[]{:S(2)}) async-start(bf16[8,320,128]{2,1,0:T(8,128)(2,1)} %get-tuple-element.160), calls=%async_computation.4 | async-start | bytes 1310720 | tf_op jit(solution)/shard_map/all_to_all | solution.py:908
  208.8 30.6 %collective-permute-start.26 = (bf16[1024,512]{1,0:T(8,128)(2,1)}, bf16[1024,512]{1,0:T(8,128)(2,1)S(1)}, u32[]{:S(2)}, u32[]{:S(2)}) collective-permute-start(bf16[1024,512]{1,0:T(8,128)(2,1)} %get-tuple-element.158.refs_1_), channel_id=1, source_target_pairs={{0,2},{1,3},{2,0},{3,1},{4,6},{5,7},{6,4},{7,5},{8,10},{9,11},{10,... | collective-permute-start | bytes 3145736 | tf_op jit(solution)/shard_map/ppermute | solution.py:722
  227.1 11.3 %collective-permute-start.28 = (bf16[192,512]{1,0:T(8,128)(2,1)S(1)}, bf16[192,512]{1,0:T(8,128)(2,1)S(1)}, u32[]{:S(2)}, u32[]{:S(2)}) collective-permute-start(bf16[192,512]{1,0:T(8,128)(2,1)S(1)} %get-tuple-element.163.refs_2_), channel_id=1, source_target_pairs={{0,16},{4,20},{8,24},{12,28},{16,0},{20,4},{24,8},{28,12},{1,17},{... | collective-permute-start | bytes 589832 | tf_op jit(solution)/shard_map/ppermute | solution.py:722
  227.2 11.2 %collective-permute-start.29 = (bf16[192,512]{1,0:T(8,128)(2,1)S(1)}, bf16[192,512]{1,0:T(8,128)(2,1)S(1)}, u32[]{:S(2)}, u32[]{:S(2)}) collective-permute-start(bf16[192,512]{1,0:T(8,128)(2,1)S(1)} %get-tuple-element.163.refs_2_), channel_id=1, source_target_pairs={{0,4},{4,0},{8,12},{12,8},{16,20},{20,16},{24,28},{28,24},{1,5},{5... | collective-permute-start | bytes 589832 | tf_op jit(solution)/shard_map/ppermute | solution.py:722
  228.7 10.7 %collective-permute-start.30 = (bf16[192,512]{1,0:T(8,128)(2,1)S(1)}, bf16[192,512]{1,0:T(8,128)(2,1)S(1)}, u32[]{:S(2)}, u32[]{:S(2)}) collective-permute-start(bf16[192,512]{1,0:T(8,128)(2,1)S(1)} %get-tuple-element.163.refs_2_), channel_id=1, source_target_pairs={{0,8},{4,12},{8,0},{12,4},{16,24},{20,28},{24,16},{28,20},{1,9},{5... | collective-permute-start | bytes 589832 | tf_op jit(solution)/shard_map/ppermute | solution.py:722
  245.2 21.3 %collective-permute-start.32 = (bf16[1024,512]{1,0:T(8,128)(2,1)S(1)}, bf16[1024,512]{1,0:T(8,128)(2,1)S(1)}, u32[]{:S(2)}, u32[]{:S(2)}) collective-permute-start(bf16[1024,512]{1,0:T(8,128)(2,1)S(1)} %get-tuple-element.165.refs_1_), channel_id=1, source_target_pairs={{0,1},{1,0},{2,3},{3,2},{4,5},{5,4},{6,7},{7,6},{8,9},{9,8},{10,11... | collective-permute-start | bytes 3145736 | tf_op jit(solution)/shard_map/ppermute | solution.py:722
  252.5 7.8 %collective-permute-start.34 = (bf16[192,512]{1,0:T(8,128)(2,1)S(1)}, bf16[192,512]{1,0:T(8,128)(2,1)S(1)}, u32[]{:S(2)}, u32[]{:S(2)}) collective-permute-start(bf16[192,512]{1,0:T(8,128)(2,1)S(1)} %get-tuple-element.169.refs_4_), channel_id=1, source_target_pairs={{0,4},{4,0},{8,12},{12,8},{16,20},{20,16},{24,28},{28,24},{1,5},{5... | collective-permute-start | bytes 589832 | tf_op jit(solution)/shard_map/ppermute | solution.py:722
  253.7 9.6 %collective-permute-start.35 = (bf16[192,512]{1,0:T(8,128)(2,1)S(1)}, bf16[192,512]{1,0:T(8,128)(2,1)S(1)}, u32[]{:S(2)}, u32[]{:S(2)}) collective-permute-start(bf16[192,512]{1,0:T(8,128)(2,1)S(1)} %collective-permute-done.31.refs_1_.refs_2_.refs_8_), channel_id=1, source_target_pairs={{0,4},{4,0},{8,12},{12,8},{16,20},{20,16},{24,28},{28,24},{1,5},{5... | collective-permute-start | bytes 589832 | tf_op jit(solution)/shard_map/ppermute | solution.py:722
  (51 other events, 351.3 us)

commit v2 on v1

--- a/solution.py
+++ b/solution.py
@@ -599,22 +599,26 @@
 
 
 def sum_kernel(own_ref, a_ref, b_ref, c_ref, out_ref):
-    out_ref[...] = own_ref[...] + a_ref[...].astype(F32) + b_ref[...].astype(F32) + c_ref[...].astype(F32)
-
-
-def pack_kernel(own1_ref, got_ref, packed_ref, total_ref):
-    first = own1_ref[...]
-    ways = own1_ref.shape[1] // got_ref.shape[2]
+    total = own_ref[...] + a_ref[...].astype(F32) + b_ref[...].astype(F32) + c_ref[...].astype(F32)
+    out_ref[...] = total.astype(out_ref.dtype)
+
+
+def add_kernel(a_ref, b_ref, out_ref):
+    out_ref[...] = (a_ref[...].astype(F32) + b_ref[...].astype(F32)).astype(out_ref.dtype)
+
+
+def pack_kernel(got_ref, packed_ref, total_ref):
+    ways = packed_ref.shape[2] // got_ref.shape[2]
     rows, lanes = got_ref.shape[1] - 2 * 16 * ways, got_ref.shape[2]
     value = total = 0.0
     for b in range(got_ref.shape[0]):
         value = value + got_ref[b, 0:rows, :].astype(F32)
         total = total + join_small(got_ref.at[b, rows:], total_ref.shape[1])
     total_ref[...] = total
-    edge = own1_ref.shape[0]
-    packed_ref[0:edge, :] = first.astype(packed_ref.dtype)
     for c in range(ways):
-        packed_ref[edge:, c * lanes : (c + 1) * lanes] = value[c * (rows // ways) : (c + 1) * (rows // ways)].astype(packed_ref.dtype)
+        part = value[c * (rows // ways) : (c + 1) * (rows // ways)].astype(packed_ref.dtype)
+        for b in range(packed_ref.shape[0]):
+            packed_ref[b, :, c * lanes : (c + 1) * lanes] = part
 
 
 def add_one_kernel(a_ref, b_ref, small_ref, other_ref, out_ref, total_ref):
@@ -623,23 +627,23 @@
 
 
 def spread_kernel(count, ids_ref, small_ref, *refs):
-    blocks = refs[:count]
-    qkv_ref, qv_ref, out_ref, ob_ref, up_ref, ub_ref, down_ref, db_ref, alpha_ref, turned_ref, second_ref = refs[count:]
+    firsts, seconds = refs[:count], refs[count]
+    qkv_ref, qv_ref, out_ref, ob_ref, up_ref, ub_ref, down_ref, db_ref, alpha_ref, turned_ref, second_ref = refs[count + 1 :]
     me, tensor = ids_ref[0], ids_ref[1]
     lanes = out_ref.shape[0]
-    for j, ref in enumerate(blocks):
+    for j in range(count):
         slot = lax.bitwise_xor(me % count, j)
         first = 0
         for out in (up_ref, turned_ref, out_ref):
             size = out.shape[0] // count
-            out[pl.ds(pl.multiple_of(slot * size, 8), size), :] = ref[first : first + size, :].astype(F32)
+            out[pl.ds(pl.multiple_of(slot * size, 8), size), :] = firsts[j][first : first + size, :].astype(F32)
             first += size
         size = qkv_ref.shape[1] // count
-        rest = ref.shape[0] - first
-        for c in range(ref.shape[1] // lanes):
-            second_ref[c * rest : (c + 1) * rest, :] = ref[first:, c * lanes : (c + 1) * lanes].astype(F32)
+        rest = seconds.shape[1]
+        for c in range(seconds.shape[2] // lanes):
+            second_ref[c * rest : (c + 1) * rest, :] = seconds[j, :, c * lanes : (c + 1) * lanes].astype(F32)
         for c in range(3):
-            qkv_ref[c, pl.ds(pl.multiple_of(slot * size, 8), size), :] = second_ref[c * size : (c + 1) * size, :]
+            qkv_ref[c, j * size : (j + 1) * size, :] = second_ref[c * size : (c + 1) * size, :]
     down_ref[...] = turned_ref[...].T
     ub_ref[...] = small_ref[pl.ds(tensor, 1), :]
     ob_ref[...] = small_ref[4:5, :]
@@ -844,13 +848,6 @@
     def relay(value, deps):
         return call(lambda *refs: None, (value,), [shape(value.shape, value.dtype)], ins_any=1, outs_any=1, aliases={0: 0}, deps=deps, us=0.1)[0]
 
-    def gather(own):
-        y0, r4, r2 = across("dp", 1, own), across("dp", 4, own), across("dp", 2, own)
-        r4 = relay(r4, (y0, r2))
-        y4, r6 = across("dp", 1, r4), across("dp", 2, r4)
-        r2 = relay(r2, (y4, r6))
-        return [own, y0, r2, across("dp", 1, r2), r4, y4, r6, across("dp", 1, r6)]
-
     keep1 = keep1.reshape(half * blocks, bundle, width)
     send1 = send1.reshape(half * blocks, bundle, width)
     got = across("tensor", 1, send1)
@@ -910,12 +907,20 @@
     gx_far = across("tensor", 2, gx_own)
     gx_core = across("tensor", 1, gx_own)
     y_both = across("tensor", 1, y_late)
-    own1 = call(sum_kernel, (own1, *got1), [shape(own1.shape, F32)], deps=(gx_own,), us=C["part"])[0]
+    kind = BF if groups <= blocks else F32
+    own1 = call(sum_kernel, (own1, *got1), [shape(own1.shape, kind)], deps=(gx_own,), us=C["part"])[0]
+    bit = blocks
+    while bit < groups:
+        kind = BF if 2 * bit == groups else F32
+        own1 = call(add_kernel, (own1, across("dp", bit, own1)), [shape(own1.shape, kind)])[0]
+        bit *= 2
+    a1, a4, a2 = across("dp", 1, own1), across("dp", 4, own1), across("dp", 2, own1)
     output = widen(2, y_late, y_both, output, deps=(own1,))
     gx_grad = widen(0, gx_own, gx_core, deps=(output,))
-    kind = BF if groups <= blocks else F32
+    spread_out = groups <= blocks
     own, small = call(
-        pack_kernel, (own1, shared), [shape((bundle + share // 4, width), kind), bare], deps=(gx_grad,), us=C["halve"]
+        pack_kernel, (shared,), [shape((blocks if spread_out else 1, share // 4, width), BF if spread_out else F32), bare],
+        deps=(gx_grad, a1, a4, a2), us=C["halve"],
     )
     bit = blocks
     while bit < groups:
@@ -924,8 +929,14 @@
             add_one_kernel, (own, across("dp", bit, own), small, across("dp", bit, small)), [shape(own.shape, kind), bare]
         )
         bit *= 2
-    gathered = gather(own)
-    gx_far = relay(gx_far, (gathered[blocks - 2],))
+    if not spread_out:
+        own = jnp.broadcast_to(own, (blocks, *own.shape[1:]))
+    second = lax.all_to_all(own, "dp", 0, 0, tiled=True, axis_index_groups=ranks)
+    a4 = relay(a4, (own,))
+    a2 = relay(a2, (own,))
+    a5, a6, a3 = across("dp", 1, a4), across("dp", 2, a4), across("dp", 1, a2)
+    gathered = [own1, a1, a2, a3, a4, a5, a6, across("dp", 1, a6), second]
+    gx_far = relay(gx_far, (a6, a5, a3))
     gx_both = across("tensor", 1, gx_far)
     qkv_grad, qv_grad, out_grad, ob_grad, up_grad, ub_grad, down_grad, db_grad, alphas = call(
         functools.partial(spread_kernel, blocks), (ids, small, *gathered),

time: 275 us -> 264 us (0.960)
  waiting for transfers between devices: 69.9 us -> 50.2 us
  starting transfers between devices: 52.5 us -> 59.7 us
    ppermute x36, waiting for transfers between devices: 43.4 us -> 25.9 us  [across(): return lax.ppermute(value, axis, [(i, i ^ bit) for i in range(count)])]
    all_to_all x0 -> x1, starting transfers between devices: none -> 4.15 us  [per_device(): lax.all_to_all(own, 'dp', 0, 0, tiled=True, axis_index_groups=ranks)]
    ppermute x36, starting transfers between devices: 26.9 us -> 29.9 us  [across(): return lax.ppermute(value, axis, [(i, i ^ bit) for i in range(count)])]
    unnamed x84 -> x80, local copies, waits for them, and re-layouts: 16.3 us -> 16.2 us
  transfers between devices with their start and end apart: 41 -> 42, of which waited for: 15 -> 14; matrix products, arithmetic and copies ran while one was open for 1% -> 1% of each run, Pallas kernels for 35% -> 37%
where the time goes in v2:
time: 264 us; the launch traced here: 259 us
  Pallas kernels  128 us (48%)
  starting transfers between devices  59.7 us (23%)
  waiting for transfers between devices  50.2 us (19%)
  local copies, waits for them, and re-layouts  18.9 us (7%)
    pallas_call x25, Pallas kernels, call(): pl.pallas_call(body, out_shape=[*outs, shape((8, LANES), F32)], in_specs=...  117 us
    ppermute x36, starting transfers between devices, across(): return lax.ppermute(value, axis, [(i, i ^ bit) for i in range(count)])  29.9 us
    ppermute x36, waiting for transfers between devices, across(): return lax.ppermute(value, axis, [(i, i ^ bit) for i in range(count)])  25.9 us
    all_to_all x4, starting transfers between devices, exchange(): lax.all_to_all(rows_out.reshape(groups, rows // groups, width), 'dp', 0,...  22.1 us
    all_to_all x4, waiting for transfers between devices, exchange(): lax.all_to_all(rows_out.reshape(groups, rows // groups, width), 'dp', 0,...  18.7 us
    unnamed x80, local copies, waits for them, and re-layouts  16.2 us
    pallas_call x1, Pallas kernels, per_device(): by_micro(functools.partial(route_kernel, groups), 0, [shape((rows, width)...  6.25 us
    all_to_all x1, waiting for transfers between devices, per_device(): lax.all_to_all(shared, 'dp', 0, 0, tiled=True, axis_index_groups=ranks)  5.62 us
  transfers between devices with their start and end apart: 42, of which 14 were waited for; matrix products, arithmetic and copies ran while one was open for 1% of the time, Pallas kernels for 37%

profile of v2, /device:TPU:0, one launch (start us, length us, event | category | flops | bytes accessed | tf_op | source)
XLA Modules:
  0.0 258.8 jit_solution(13664773066480402745)
XLA Ops:
  1.2 6.2 %shard_map.212 = (bf16[1024,512]{1,0:T(8,128)(2,1)}, s32[8,128]{1,0:T(8,128)}, s32[1024,128]{1,0:T(8,128)}) custom-call(s32[2]{0:T(128)} %pad_add_fusion.ids_ref.refs_0_, s32[4,8192]{1,0:T(4,128)} %src_ref.3, bf16[4,1024,512]{2,1,0:T(8,128)(2,1)} %x_ref.1), custom_call_target="tpu_custom_call" | custom-call | flops 6000000000 | tf_op jit(solution)/shard_map/pallas_call | solution.py:751
  7.5 7.3 %all-to-all-start = ((bf16[8,128,512]{2,1,0:T(8,128)(2,1)}), bf16[8,128,512]{2,1,0:T(8,128)(2,1)S(1)}, u32[]{:S(2)}, u32[]{:S(2)}) async-start(bf16[8,128,512]{2,1,0:T(8,128)(2,1)} %bitcast.21), calls=%async_computation | async-start | bytes 2097152 | tf_op jit(solution)/shard_map/all_to_all | solution.py:757
  18.5 4.9 %shard_map.213 = (bf16[1024,512]{1,0:T(8,128)(2,1)}, s32[8,1024]{1,0:T(8,128)}, s32[1024,128]{1,0:T(8,128)}) custom-call(s32[2]{0:T(128)} %pad_add_fusion.ids_ref.refs_0_, s32[4,8192]{1,0:T(4,128)} %src_ref.3, bf16[4,1024,512]{2,1,0:T(8,128)(2,1)} %g_ref.1, s32[8,128]{1,0:T(8,128)} %get-tuple-element.96.srow_ref), custom_call_target="tpu_custom_call" | custom-call | flops 6000000000 | tf_op jit(solution)/shard_map/pallas_call | solution.py:760
  23.4 3.5 %collective-permute-done.1.refs_5_.refs_3_.refs_4_ = bf16[8,128]{1,0:T(8,128)(2,1)S(1)} collective-permute-done((bf16[8,128]{1,0:T(8,128)(2,1)S(1)}, bf16[8,128]{1,0:T(8,128)(2,1)S(1)}, u32[]{:S(2)}, u32[]{:S(2)}) %collective-permute-start.1) | collective-permute-done | bytes 2080 | tf_op jit(solution)/shard_map/ppermute | solution.py:726
  34.3 6.2 %all-to-all-done = bf16[8,128,512]{2,1,0:T(8,128)(2,1)S(1)} async-done(((bf16[8,128,512]{2,1,0:T(8,128)(2,1)}), bf16[8,128,512]{2,1,0:T(8,128)(2,1)S(1)}, u32[]{:S(2)}, u32[]{:S(2)}) %all-to-all-start) | async-done | bytes 1048608 | tf_op jit(solution)/shard_map/all_to_all | solution.py:757
  40.6 3.9 %all-to-all-start.2 = ((bf16[8,128,512]{2,1,0:T(8,128)(2,1)}), bf16[8,128,512]{2,1,0:T(8,128)(2,1)S(1)}, u32[]{:S(2)}, u32[]{:S(2)}) async-start(bf16[8,128,512]{2,1,0:T(8,128)(2,1)} %bitcast.19), calls=%async_computation.2 | async-start | bytes 2097152 | tf_op jit(solution)/shard_map/all_to_all | solution.py:757
  44.5 18.6 %shard_map.214 = (f32[8,1024]{1,0:T(8,128)}, bf16[1024,512]{1,0:T(8,128)(2,1)}, bf16[1024,512]{1,0:T(8,128)(2,1)}, bf16[1024,512]{1,0:T(8,128)(2,1)}, bf16[1024,...) custom-call(s32[2]{0:T(128)} %pad_add_fusion.ids_ref.refs_0_, ...), custom_call_target="tpu_custom_call" | custom-call | flops 19000000512 | tf_op jit(solution)/shard_map/pallas_call | solution.py:694
  66.9 10.5 %shard_map.215 = (bf16[1024,512]{1,0:T(8,128)(2,1)}, f32[1024,512]{1,0:T(8,128)}, f32[8,128]{1,0:T(8,128)}) custom-call(f32[2]{0:T(128)} %refs_1_.1, bf16[8,128]{1,0:T(8,128)(2,1)} %copy-done.22, bf16[8,128]{1,0:T(8,128)(2,1)} %copy-done.38, bf16[8,128]{1,0:T(8,128)(2,1)} %copy-done.37, bf16[8,128]{1,0:T(8,128)(2,1)} %copy-done.39, ...), custom_call_target="tpu_custom_call" | custom-call | flops 5000000000 | tf_op jit(solution)/shard_map/pallas_call | solution.py:694
  78.4 21.7 %shard_map.216 = (f32[8,512]{1,0:T(8,128)}, bf16[1024,512]{1,0:T(8,128)(2,1)}, f32[1024,512]{1,0:T(8,128)}, f32[2,8,144,512]{3,2,1,0:T(8,128)}, bf16[2,8,144,512]{3,2,1,0:T(8,128)(2,1)}, /*index=5*/f32[8,128]{1,0:T(8,128)}) custom-call(s32[2]{0:T(128)} %pad_add_fusion.ids_ref.refs_0_, f32[2]{0:T(128)} %refs_1_.1, bf16[8,128]{1,0:T(8,128)(2,1)} %copy-done.22, ...), custom_call_target="tpu_custom_call" | custom-call | flops 19000000512 | tf_op jit(solution)/shard_map/pallas_call | solution.py:694
  100.3 6.2 %all-to-all-start.1 = ((bf16[8,128,512]{2,1,0:T(8,128)(2,1)}), bf16[8,128,512]{2,1,0:T(8,128)(2,1)S(1)}, u32[]{:S(2)}, u32[]{:S(2)}) async-start(bf16[8,128,512]{2,1,0:T(8,128)(2,1)} %bitcast.24), calls=%async_computation.1 | async-start | bytes 2097152 | tf_op jit(solution)/shard_map/all_to_all | solution.py:757
  106.5 2.3 copy-done.2
  114.2 11.0 %shard_map.218 = (bf16[3,1024,256]{2,1,0:T(8,128)(2,1)}, f32[8,128]{1,0:T(8,128)}) custom-call(s32[3]{0:T(128)} %dynamic-slice_reduce_fusion.refs_1_.refs_0_, f32[8,1024]{1,0:T(8,128)} %get-tuple-element.105.refs_1_, bf16[1024,512]{1,0:T(8,128)(2,1)} %get-tuple-element.110.refs_2_, bf16[1024,512]{1,0:T(8,128)(2,1)} %get-tuple-element.111.refs_3_, ...), custom_call_target="tpu_custom_call" | custom-call | flops 11000000512 | tf_op jit(solution)/shard_map/pallas_call | solution.py:694
  125.2 11.6 %shard_map.219 = (bf16[3,1024,256]{2,1,0:T(8,128)(2,1)}, f32[8,128]{1,0:T(8,128)}) custom-call(s32[3]{0:T(128)} %dynamic-slice_reduce_fusion.refs_1_.refs_0_, f32[8,1024]{1,0:T(8,128)} %get-tuple-element.105.refs_1_, bf16[1024,512]{1,0:T(8,128)(2,1)} %get-tuple-element.110.refs_2_, bf16[1024,512]{1,0:T(8,128)(2,1)} %get-tuple-element.111.refs_3_, ...), custom_call_target="tpu_custom_call" | custom-call | flops 11000000512 | tf_op jit(solution)/shard_map/pallas_call | solution.py:694
  141.9 6.7 %shard_map.221 = (f32[16,512]{1,0:T(8,128)}, f32[16,192,128]{2,1,0:T(8,128)}, bf16[17,192,128]{2,1,0:T(8,128)(2,1)}, f32[8,128]{1,0:T(8,128)}) custom-call(s32[2]{0:T(128)} %pad_add_fusion.ids_ref.refs_0_, f32[8,512]{1,0:T(8,128)} %get-tuple-element.127.refs_1_, bf16[3,1024,256]{2,1,0:T(8,128)(2,1)} %get-tuple-element.128.refs_2_, ...), custom_call_target="tpu_custom_call" | custom-call | flops 200000000 | tf_op jit(solution)/shard_map/pallas_call | solution.py:694
  155.9 7.8 %shard_map.223 = (bf16[1024,512]{1,0:T(8,128)(2,1)}, f32[8,128]{1,0:T(8,128)}) custom-call(s32[2]{0:T(128)} %pad_add_fusion.ids_ref.refs_0_, s32[8,1024]{1,0:T(8,128)} %get-tuple-element.97.refs_6_.refs_1_, bf16[3,1024,256]{2,1,0:T(8,128)(2,1)} %get-tuple-element.128.refs_2_, bf16[3,1024,256]{2,1,0:T(8,128)(2,1)} %get-tuple-element.129.refs_3_, ...), custom_call_target="tpu_custom_call" | custom-call | flops 20000000000 | tf_op jit(solution)/shard_map/pallas_call | solution.py:694
  163.7 4.8 %all-to-all-start.3 = ((bf16[8,128,512]{2,1,0:T(8,128)(2,1)}), bf16[8,128,512]{2,1,0:T(8,128)(2,1)S(1)}, u32[]{:S(2)}, u32[]{:S(2)}) async-start(bf16[8,128,512]{2,1,0:T(8,128)(2,1)} %bitcast.22), calls=%async_computation.3 | async-start | bytes 2097152 | tf_op jit(solution)/shard_map/all_to_all | solution.py:757
  173.1 6.2 %collective-permute-done.18.refs_1_ = bf16[4,144,512]{2,1,0:T(8,128)(2,1)S(1)} collective-permute-done((bf16[4,144,512]{2,1,0:T(8,128)(2,1)}, bf16[4,144,512]{2,1,0:T(8,128)(2,1)S(1)}, u32[]{:S(2)}, u32[]{:S(2)}) %collective-permute-start.18) | collective-permute-done | bytes 589856 | tf_op jit(solution)/shard_map/ppermute | solution.py:726
  181.6 2.4 collective-permute-start.23
  184.6 3.9 %shard_map.227 = (f32[4,1024,512]{2,1,0:T(8,128)}, f32[8,128]{1,0:T(8,128)S(1)}) custom-call(s32[2]{0:T(128)S(1)} %copy-done.4, bf16[1024,512]{1,0:T(8,128)(2,1)} %get-tuple-element.124.refs_1_, bf16[1024,512]{1,0:T(8,128)(2,1)} %collective-permute-done.21.refs_2_, f32[8,128]{1,0:T(8,128)S(1)} %get-tuple-element.142.refs_1_.refs_3_), custom_call_target="tpu_custom_call" | custom-call | flops 5000000000 | tf_op jit(solution)/shard_map/pallas_call | solution.py:694
  189.4 12.5 %all-to-all-done.3 = bf16[8,128,512]{2,1,0:T(8,128)(2,1)S(1)} async-done(((bf16[8,128,512]{2,1,0:T(8,128)(2,1)}), bf16[8,128,512]{2,1,0:T(8,128)(2,1)S(1)}, u32[]{:S(2)}, u32[]{:S(2)}) %all-to-all-start.3) | async-done | bytes 1048608 | tf_op jit(solution)/shard_map/all_to_all | solution.py:757
  203.0 2.3 shard_map.229
  205.3 3.5 %all-to-all-start.4 = ((bf16[8,320,128]{2,1,0:T(8,128)(2,1)}), bf16[8,320,128]{2,1,0:T(8,128)(2,1)S(1)}, u32[]{:S(2)}, u32[]{:S(2)}) async-start(bf16[8,320,128]{2,1,0:T(8,128)(2,1)} %get-tuple-element.161), calls=%async_computation.4 | async-start | bytes 1310720 | tf_op jit(solution)/shard_map/all_to_all | solution.py:905
  211.4 2.8 %collective-permute-start.27 = (bf16[144,512]{1,0:T(8,128)(2,1)S(1)}, bf16[144,512]{1,0:T(8,128)(2,1)S(1)}, u32[]{:S(2)}, u32[]{:S(2)}) collective-permute-start(bf16[144,512]{1,0:T(8,128)(2,1)S(1)} %get-tuple-element.160.refs_2_), channel_id=1, source_target_pairs={{0,16},{4,20},{8,24},{12,28},{16,0},{20,4},{24,8},{28,12},{1,17},{... | collective-permute-start | bytes 442376 | tf_op jit(solution)/shard_map/ppermute | solution.py:726
  217.2 3.9 %shard_map.231 = (f32[4,1024,512]{2,1,0:T(8,128)}, f32[8,128]{1,0:T(8,128)S(1)}) custom-call(s32[2]{0:T(128)S(1)} %copy-done.4, bf16[1024,512]{1,0:T(8,128)(2,1)S(1)} %get-tuple-element.143.refs_1_, bf16[1024,512]{1,0:T(8,128)(2,1)} %collective-permute-done.20.refs_2_, f32[4,1024,512]{2,1,0:T(8,128)} %get-tuple-element.144.refs_3_, ...), custom_call_target="tpu_custom_call", output_to_operand_aliasing={{0}: (3, {})} | custom-call | flops 5000000000 | tf_op jit(solution)/shard_map/pallas_call | solution.py:694
  221.1 3.9 %shard_map.232 = (f32[4,1024,512]{2,1,0:T(8,128)}, f32[8,128]{1,0:T(8,128)S(1)}) custom-call(s32[2]{0:T(128)S(1)} %copy-done.4, bf16[1024,512]{1,0:T(8,128)(2,1)} %get-tuple-element.159.refs_1_, bf16[1024,512]{1,0:T(8,128)(2,1)} %collective-permute-done.28.refs_2_, f32[8,128]{1,0:T(8,128)S(1)} %get-tuple-element.162.refs_3_), custom_call_target="tpu_custom_call" | custom-call | flops 5000000000 | tf_op jit(solution)/shard_map/pallas_call | solution.py:694
  225.0 5.6 %all-to-all-done.4.refs_0_ = bf16[8,320,128]{2,1,0:T(8,128)(2,1)S(1)} async-done(((bf16[8,320,128]{2,1,0:T(8,128)(2,1)}), bf16[8,320,128]{2,1,0:T(8,128)(2,1)S(1)}, u32[]{:S(2)}, u32[]{:S(2)}) %all-to-all-start.4) | async-done | bytes 655392 | tf_op jit(solution)/shard_map/all_to_all | solution.py:905
  230.6 2.8 %collective-permute-done.27.refs_3_.refs_0_ = bf16[144,512]{1,0:T(8,128)(2,1)S(1)} collective-permute-done((bf16[144,512]{1,0:T(8,128)(2,1)S(1)}, bf16[144,512]{1,0:T(8,128)(2,1)S(1)}, u32[]{:S(2)}, u32[]{:S(2)}) %collective-permute-start.27) | collective-permute-done | bytes 147488 | tf_op jit(solution)/shard_map/ppermute | solution.py:726
  236.3 4.1 %all-to-all-start.5 = ((bf16[8,48,512]{2,1,0:T(8,128)(2,1)}), bf16[8,48,512]{2,1,0:T(8,128)(2,1)S(1)}, u32[]{:S(2)}, u32[]{:S(2)}) async-start(bf16[8,48,512]{2,1,0:T(8,128)(2,1)} %get-tuple-element.171), calls=%async_computation.5 | async-start | bytes 786432 | tf_op jit(solution)/shard_map/all_to_all | solution.py:934
  241.0 2.4 collective-permute-done.33.refs_3_.refs_5_
  245.3 6.1 %collective-permute-done.35.refs_9_ = bf16[144,512]{1,0:T(8,128)(2,1)S(1)} collective-permute-done((bf16[144,512]{1,0:T(8,128)(2,1)S(1)}, bf16[144,512]{1,0:T(8,128)(2,1)S(1)}, u32[]{:S(2)}, u32[]{:S(2)}) %collective-permute-start.35) | collective-permute-done | bytes 147488 | tf_op jit(solution)/shard_map/ppermute | solution.py:726
  251.5 2.6 %shard_map.238 = (f32[3,512,128]{2,1,0:T(8,128)}, f32[2,128]{1,0:T(2,128)}, f32[128,512]{1,0:T(8,128)}, f32[1,512]{1,0:T(1,128)}, f32[512,512]{1,0:T(8,128)}, /*...) custom-call(s32[2]{0:T(128)S(1)} %copy-done.4, ...), custom_call_target="tpu_custom_call" | custom-call | flops 3000000000 | tf_op jit(solution)/shard_map/pallas_call | solution.py:694
  254.7 3.9 %shard_map.237 = (f32[4,1024,512]{2,1,0:T(8,128)}, f32[8,128]{1,0:T(8,128)}) custom-call(s32[2]{0:T(128)S(1)} %copy-done.4, bf16[1024,512]{1,0:T(8,128)(2,1)S(1)} %get-tuple-element.167.refs_1_, bf16[1024,512]{1,0:T(8,128)(2,1)} %collective-permute-done.34.refs_2_, f32[4,1024,512]{2,1,0:T(8,128)} %get-tuple-element.168.refs_3_), custom_call_target="tpu_custom_call", output_to_operand_aliasing={{0}: (3, {})} | custom-call | flops 5000000000 | tf_op jit(solution)/shard_map/pallas_call | solution.py:694
  (167 shorter events, 55.4 us)
Async XLA Ops:
  7.5 33.0 %all-to-all-start = ((bf16[8,128,512]{2,1,0:T(8,128)(2,1)}), bf16[8,128,512]{2,1,0:T(8,128)(2,1)S(1)}, u32[]{:S(2)}, u32[]{:S(2)}) async-start(bf16[8,128,512]{2,1,0:T(8,128)(2,1)} %bitcast.21), calls=%async_computation | async-start | bytes 2097152 | tf_op jit(solution)/shard_map/all_to_all | solution.py:757
  14.8 13.5 %collective-permute-start.2 = (bf16[3,512,128]{2,1,0:T(8,128)(2,1)S(1)}, bf16[3,512,128]{2,1,0:T(8,128)(2,1)}, u32[]{:S(2)}, u32[]{:S(2)}) collective-permute-start(bf16[3,512,128]{2,1,0:T(8,128)(2,1)S(1)} %copy-done.31), channel_id=1, source_target_pairs={{0,2},{1,3},{2,0},{3,1},{4,6},{5,7},{6,4},{7,5},{8,10},{9,11},{10,... | collective-permute-start | bytes 1179656 | tf_op jit(solution)/shard_map/ppermute | solution.py:726
  16.3 15.9 %collective-permute-start.5 = (bf16[3,512,128]{2,1,0:T(8,128)(2,1)S(1)}, bf16[3,512,128]{2,1,0:T(8,128)(2,1)S(1)}, u32[]{:S(2)}, u32[]{:S(2)}) collective-permute-start(bf16[3,512,128]{2,1,0:T(8,128)(2,1)S(1)} %copy-done.31), channel_id=1, source_target_pairs={{0,1},{1,0},{2,3},{3,2},{4,5},{5,4},{6,7},{7,6},{8,9},{9,8},{10,11... | collective-permute-start | bytes 1179656 | tf_op jit(solution)/shard_map/ppermute | solution.py:726
  16.5 10.4 %collective-permute-start.1 = (bf16[8,128]{1,0:T(8,128)(2,1)S(1)}, bf16[8,128]{1,0:T(8,128)(2,1)S(1)}, u32[]{:S(2)}, u32[]{:S(2)}) collective-permute-start(bf16[8,128]{1,0:T(8,128)(2,1)S(1)} %maximum_maximum_fusion.refs_3_.refs_1_.refs_2_), channel_id=1, source_target_pairs={{0,2},{1,3},{2,0},{3,1},{4,6},{5,7},{6,4},{7,5},{8,10},{9,11},{10,... | collective-permute-start | bytes 6152 | tf_op jit(solution)/shard_map/ppermute | solution.py:726
  17.0 11.2 %collective-permute-start.3 = (bf16[128,512]{1,0:T(8,128)(2,1)S(1)}, bf16[128,512]{1,0:T(8,128)(2,1)S(1)}, u32[]{:S(2)}, u32[]{:S(2)}) collective-permute-start(bf16[128,512]{1,0:T(8,128)(2,1)S(1)} %copy-done.33), channel_id=1, source_target_pairs={{0,2},{1,3},{2,0},{3,1},{4,6},{5,7},{6,4},{7,5},{8,10},{9,11},{10,... | collective-permute-start | bytes 393224 | tf_op jit(solution)/shard_map/ppermute | solution.py:726
  28.3 16.2 %collective-permute-start.6 = (bf16[3,512,128]{2,1,0:T(8,128)(2,1)}, bf16[3,512,128]{2,1,0:T(8,128)(2,1)}, u32[]{:S(2)}, u32[]{:S(2)}) collective-permute-start(bf16[3,512,128]{2,1,0:T(8,128)(2,1)} %collective-permute-done.2.refs_12_.refs_7_), channel_id=1, source_target_pairs={{0,1},{1,0},{2,3},{3,2},{4,5},{5,4},{6,7},{7,6},{8,9},{9,8},{10,11... | collective-permute-start | bytes 1179656 | tf_op jit(solution)/shard_map/ppermute | solution.py:726
  31.9 32.4 %collective-permute-start.9 = (bf16[512,512]{1,0:T(8,128)(2,1)S(1)}, bf16[512,512]{1,0:T(8,128)(2,1)}, u32[]{:S(2)}, u32[]{:S(2)}) collective-permute-start(bf16[512,512]{1,0:T(8,128)(2,1)S(1)} %copy-done.27), channel_id=1, source_target_pairs={{0,1},{1,0},{2,3},{3,2},{4,5},{5,4},{6,7},{7,6},{8,9},{9,8},{10,11... | collective-permute-start | bytes 1572872 | tf_op jit(solution)/shard_map/ppermute | solution.py:726
  32.2 30.9 %collective-permute-start.10 = (bf16[512,512]{1,0:T(8,128)(2,1)S(1)}, bf16[512,512]{1,0:T(8,128)(2,1)}, u32[]{:S(2)}, u32[]{:S(2)}) collective-permute-start(bf16[512,512]{1,0:T(8,128)(2,1)S(1)} %copy-done.27), channel_id=1, source_target_pairs={{0,2},{1,3},{2,0},{3,1},{4,6},{5,7},{6,4},{7,5},{8,10},{9,11},{10,... | collective-permute-start | bytes 1572872 | tf_op jit(solution)/shard_map/ppermute | solution.py:726
  33.7 29.4 %collective-permute-start.11 = (bf16[512,512]{1,0:T(8,128)(2,1)S(1)}, bf16[512,512]{1,0:T(8,128)(2,1)}, u32[]{:S(2)}, u32[]{:S(2)}) collective-permute-start(bf16[512,512]{1,0:T(8,128)(2,1)S(1)} %copy-done.28), channel_id=1, source_target_pairs={{0,2},{1,3},{2,0},{3,1},{4,6},{5,7},{6,4},{7,5},{8,10},{9,11},{10,... | collective-permute-start | bytes 1572872 | tf_op jit(solution)/shard_map/ppermute | solution.py:726
  34.3 30.0 %collective-permute-start.13 = (bf16[512,512]{1,0:T(8,128)(2,1)S(1)}, bf16[512,512]{1,0:T(8,128)(2,1)}, u32[]{:S(2)}, u32[]{:S(2)}) collective-permute-start(bf16[512,512]{1,0:T(8,128)(2,1)S(1)} %copy-done.28), channel_id=1, source_target_pairs={{0,1},{1,0},{2,3},{3,2},{4,5},{5,4},{6,7},{7,6},{8,9},{9,8},{10,11... | collective-permute-start | bytes 1572872 | tf_op jit(solution)/shard_map/ppermute | solution.py:726
  40.6 36.8 %all-to-all-start.2 = ((bf16[8,128,512]{2,1,0:T(8,128)(2,1)}), bf16[8,128,512]{2,1,0:T(8,128)(2,1)S(1)}, u32[]{:S(2)}, u32[]{:S(2)}) async-start(bf16[8,128,512]{2,1,0:T(8,128)(2,1)} %bitcast.19), calls=%async_computation.2 | async-start | bytes 2097152 | tf_op jit(solution)/shard_map/all_to_all | solution.py:757
  100.3 36.6 %all-to-all-start.1 = ((bf16[8,128,512]{2,1,0:T(8,128)(2,1)}), bf16[8,128,512]{2,1,0:T(8,128)(2,1)S(1)}, u32[]{:S(2)}, u32[]{:S(2)}) async-start(bf16[8,128,512]{2,1,0:T(8,128)(2,1)} %bitcast.24), calls=%async_computation.1 | async-start | bytes 2097152 | tf_op jit(solution)/shard_map/all_to_all | solution.py:757
  112.2 37.0 %collective-permute-start.17 = (bf16[8,144,512]{2,1,0:T(8,128)(2,1)}, bf16[8,144,512]{2,1,0:T(8,128)(2,1)}, u32[]{:S(2)}, u32[]{:S(2)}) collective-permute-start(bf16[8,144,512]{2,1,0:T(8,128)(2,1)} %get-tuple-element.126), channel_id=1, source_target_pairs={{0,4},{4,0},{8,12},{12,8},{16,20},{20,16},{24,28},{28,24},{1,5},{5... | collective-permute-start | bytes 3538952 | tf_op jit(solution)/shard_map/ppermute | solution.py:726
  140.4 32.7 %collective-permute-start.16 = (bf16[1024,512]{1,0:T(8,128)(2,1)}, bf16[1024,512]{1,0:T(8,128)(2,1)S(1)}, u32[]{:S(2)}, u32[]{:S(2)}) collective-permute-start(bf16[1024,512]{1,0:T(8,128)(2,1)} %get-tuple-element.124.refs_1_), channel_id=1, source_target_pairs={{0,2},{1,3},{2,0},{3,1},{4,6},{5,7},{6,4},{7,5},{8,10},{9,11},{10,... | collective-permute-start | bytes 3145736 | tf_op jit(solution)/shard_map/ppermute | solution.py:726
  141.9 42.1 %collective-permute-start.21 = (bf16[1024,512]{1,0:T(8,128)(2,1)}, bf16[1024,512]{1,0:T(8,128)(2,1)}, u32[]{:S(2)}, u32[]{:S(2)}) collective-permute-start(bf16[1024,512]{1,0:T(8,128)(2,1)} %get-tuple-element.124.refs_1_), channel_id=1, source_target_pairs={{0,1},{1,0},{2,3},{3,2},{4,5},{5,4},{6,7},{7,6},{8,9},{9,8},{10,11... | collective-permute-start | bytes 3145736 | tf_op jit(solution)/shard_map/ppermute | solution.py:726
  148.6 19.9 %collective-permute-start.19 = (bf16[17,192,128]{2,1,0:T(8,128)(2,1)}, bf16[17,192,128]{2,1,0:T(8,128)(2,1)S(1)}, u32[]{:S(2)}, u32[]{:S(2)}) collective-permute-start(bf16[17,192,128]{2,1,0:T(8,128)(2,1)} %get-tuple-element.137), channel_id=1, source_target_pairs={{0,1},{1,0},{2,3},{3,2},{4,5},{5,4},{6,7},{7,6},{8,9},{9,8},{10,11... | collective-permute-start | bytes 2506760 | tf_op jit(solution)/shard_map/ppermute | solution.py:726
  155.4 23.9 %collective-permute-start.18 = (bf16[4,144,512]{2,1,0:T(8,128)(2,1)}, bf16[4,144,512]{2,1,0:T(8,128)(2,1)S(1)}, u32[]{:S(2)}, u32[]{:S(2)}) collective-permute-start(bf16[4,144,512]{2,1,0:T(8,128)(2,1)} %get-tuple-element.134), channel_id=1, source_target_pairs={{0,2},{1,3},{2,0},{3,1},{4,6},{5,7},{6,4},{7,5},{8,10},{9,11},{10,... | collective-permute-start | bytes 1769480 | tf_op jit(solution)/shard_map/ppermute | solution.py:726
  163.7 38.2 %all-to-all-start.3 = ((bf16[8,128,512]{2,1,0:T(8,128)(2,1)}), bf16[8,128,512]{2,1,0:T(8,128)(2,1)S(1)}, u32[]{:S(2)}, u32[]{:S(2)}) async-start(bf16[8,128,512]{2,1,0:T(8,128)(2,1)} %bitcast.22), calls=%async_computation.3 | async-start | bytes 2097152 | tf_op jit(solution)/shard_map/all_to_all | solution.py:757
  171.5 17.0 %collective-permute-start.25 = (bf16[9,192,128]{2,1,0:T(8,128)(2,1)S(1)}, bf16[9,192,128]{2,1,0:T(8,128)(2,1)S(1)}, u32[]{:S(2)}, u32[]{:S(2)}) collective-permute-start(bf16[9,192,128]{2,1,0:T(8,128)(2,1)S(1)} %get-tuple-element.152), channel_id=1, source_target_pairs={{0,2},{1,3},{2,0},{3,1},{4,6},{5,7},{6,4},{7,5},{8,10},{9,11},{10,... | collective-permute-start | bytes 1327112 | tf_op jit(solution)/shard_map/ppermute | solution.py:726
  180.1 35.6 %collective-permute-start.20 = (bf16[1024,512]{1,0:T(8,128)(2,1)S(1)}, bf16[1024,512]{1,0:T(8,128)(2,1)}, u32[]{:S(2)}, u32[]{:S(2)}) collective-permute-start(bf16[1024,512]{1,0:T(8,128)(2,1)S(1)} %get-tuple-element.143.refs_1_), channel_id=1, source_target_pairs={{0,1},{1,0},{2,3},{3,2},{4,5},{5,4},{6,7},{7,6},{8,9},{9,8},{10,11... | collective-permute-start | bytes 3145736 | tf_op jit(solution)/shard_map/ppermute | solution.py:726
  180.1 28.7 %collective-permute-start.22 = (bf16[144,512]{1,0:T(8,128)(2,1)}, bf16[144,512]{1,0:T(8,128)(2,1)S(1)}, u32[]{:S(2)}, u32[]{:S(2)}) collective-permute-start(bf16[144,512]{1,0:T(8,128)(2,1)} %get-tuple-element.146), channel_id=1, source_target_pairs={{0,8},{4,12},{8,0},{12,4},{16,24},{20,28},{24,16},{28,20},{1,9},{5... | collective-permute-start | bytes 442376 | tf_op jit(solution)/shard_map/ppermute | solution.py:726
  181.6 28.7 %collective-permute-start.23 = (bf16[144,512]{1,0:T(8,128)(2,1)}, bf16[144,512]{1,0:T(8,128)(2,1)S(1)}, u32[]{:S(2)}, u32[]{:S(2)}) collective-permute-start(bf16[144,512]{1,0:T(8,128)(2,1)} %get-tuple-element.147), channel_id=1, source_target_pairs={{0,16},{4,20},{8,24},{12,28},{16,0},{20,4},{24,8},{28,12},{1,17},{... | collective-permute-start | bytes 442376 | tf_op jit(solution)/shard_map/ppermute | solution.py:726
  184.0 26.4 %collective-permute-start.24 = (bf16[144,512]{1,0:T(8,128)(2,1)S(1)}, bf16[144,512]{1,0:T(8,128)(2,1)S(1)}, u32[]{:S(2)}, u32[]{:S(2)}) collective-permute-start(bf16[144,512]{1,0:T(8,128)(2,1)S(1)} %get-tuple-element.148), channel_id=1, source_target_pairs={{0,24},{4,28},{8,16},{12,20},{16,8},{20,12},{24,0},{28,4},{1,25},{... | collective-permute-start | bytes 442376 | tf_op jit(solution)/shard_map/ppermute | solution.py:726
  205.3 15.8 %collective-permute-start.28 = (bf16[1024,512]{1,0:T(8,128)(2,1)}, bf16[1024,512]{1,0:T(8,128)(2,1)}, u32[]{:S(2)}, u32[]{:S(2)}) collective-permute-start(bf16[1024,512]{1,0:T(8,128)(2,1)} %get-tuple-element.159.refs_1_), channel_id=1, source_target_pairs={{0,1},{1,0},{2,3},{3,2},{4,5},{5,4},{6,7},{7,6},{8,9},{9,8},{10,11... | collective-permute-start | bytes 3145736 | tf_op jit(solution)/shard_map/ppermute | solution.py:726
  205.3 25.4 %all-to-all-start.4 = ((bf16[8,320,128]{2,1,0:T(8,128)(2,1)}), bf16[8,320,128]{2,1,0:T(8,128)(2,1)S(1)}, u32[]{:S(2)}, u32[]{:S(2)}) async-start(bf16[8,320,128]{2,1,0:T(8,128)(2,1)} %get-tuple-element.161), calls=%async_computation.4 | async-start | bytes 1310720 | tf_op jit(solution)/shard_map/all_to_all | solution.py:905
  208.8 31.6 %collective-permute-start.26 = (bf16[1024,512]{1,0:T(8,128)(2,1)}, bf16[1024,512]{1,0:T(8,128)(2,1)S(1)}, u32[]{:S(2)}, u32[]{:S(2)}) collective-permute-start(bf16[1024,512]{1,0:T(8,128)(2,1)} %get-tuple-element.159.refs_1_), channel_id=1, source_target_pairs={{0,2},{1,3},{2,0},{3,1},{4,6},{5,7},{6,4},{7,5},{8,10},{9,11},{10,... | collective-permute-start | bytes 3145736 | tf_op jit(solution)/shard_map/ppermute | solution.py:726
  211.4 22.0 %collective-permute-start.27 = (bf16[144,512]{1,0:T(8,128)(2,1)S(1)}, bf16[144,512]{1,0:T(8,128)(2,1)S(1)}, u32[]{:S(2)}, u32[]{:S(2)}) collective-permute-start(bf16[144,512]{1,0:T(8,128)(2,1)S(1)} %get-tuple-element.160.refs_2_), channel_id=1, source_target_pairs={{0,16},{4,20},{8,24},{12,28},{16,0},{20,4},{24,8},{28,12},{1,17},{... | collective-permute-start | bytes 442376 | tf_op jit(solution)/shard_map/ppermute | solution.py:726
  214.2 19.1 %collective-permute-start.29 = (bf16[144,512]{1,0:T(8,128)(2,1)S(1)}, bf16[144,512]{1,0:T(8,128)(2,1)S(1)}, u32[]{:S(2)}, u32[]{:S(2)}) collective-permute-start(bf16[144,512]{1,0:T(8,128)(2,1)S(1)} %get-tuple-element.160.refs_2_), channel_id=1, source_target_pairs={{0,4},{4,0},{8,12},{12,8},{16,20},{20,16},{24,28},{28,24},{1,5},{5... | collective-permute-start | bytes 442376 | tf_op jit(solution)/shard_map/ppermute | solution.py:726
  215.7 17.7 %collective-permute-start.30 = (bf16[144,512]{1,0:T(8,128)(2,1)S(1)}, bf16[144,512]{1,0:T(8,128)(2,1)S(1)}, u32[]{:S(2)}, u32[]{:S(2)}) collective-permute-start(bf16[144,512]{1,0:T(8,128)(2,1)S(1)} %get-tuple-element.160.refs_2_), channel_id=1, source_target_pairs={{0,8},{4,12},{8,0},{12,4},{16,24},{20,28},{24,16},{28,20},{1,9},{5... | collective-permute-start | bytes 442376 | tf_op jit(solution)/shard_map/ppermute | solution.py:726
  236.3 15.2 %all-to-all-start.5 = ((bf16[8,48,512]{2,1,0:T(8,128)(2,1)}), bf16[8,48,512]{2,1,0:T(8,128)(2,1)S(1)}, u32[]{:S(2)}, u32[]{:S(2)}) async-start(bf16[8,48,512]{2,1,0:T(8,128)(2,1)} %get-tuple-element.171), calls=%async_computation.5 | async-start | bytes 786432 | tf_op jit(solution)/shard_map/all_to_all | solution.py:934
  243.4 11.3 %collective-permute-start.34 = (bf16[1024,512]{1,0:T(8,128)(2,1)S(1)}, bf16[1024,512]{1,0:T(8,128)(2,1)}, u32[]{:S(2)}, u32[]{:S(2)}) collective-permute-start(bf16[1024,512]{1,0:T(8,128)(2,1)S(1)} %get-tuple-element.167.refs_1_), channel_id=1, source_target_pairs={{0,1},{1,0},{2,3},{3,2},{4,5},{5,4},{6,7},{7,6},{8,9},{9,8},{10,11... | collective-permute-start | bytes 3145736 | tf_op jit(solution)/shard_map/ppermute | solution.py:726
  243.4 8.0 %collective-permute-start.35 = (bf16[144,512]{1,0:T(8,128)(2,1)S(1)}, bf16[144,512]{1,0:T(8,128)(2,1)S(1)}, u32[]{:S(2)}, u32[]{:S(2)}) collective-permute-start(bf16[144,512]{1,0:T(8,128)(2,1)S(1)} %collective-permute-done.31.refs_1_.refs_8_), channel_id=1, source_target_pairs={{0,4},{4,0},{8,12},{12,8},{16,20},{20,16},{24,28},{28,24},{1,5},{5... | collective-permute-start | bytes 442376 | tf_op jit(solution)/shard_map/ppermute | solution.py:726
  (50 other events, 344.3 us)
